TPU v7x, 256 devices: a whole 4x4x8 slice. The times are simulated.
256 devices in a mesh: curve: 64 (over x, z, core), field: 4 (over y).
Axes of the slice: x: 4, y: 4, z: 8, core: 2. Of those that a mesh axis runs over, the one named last changes fastest.
Arguments:
- column_state: float32 [72, 48, 4096], P(None, 'field', 'curve'), may hold values from -6 to 6
- span_of: int32 [4096], P('curve'), may hold values from 0 to 63, as said below
- diffusivity: float32 [72, 8192], P(None, 'curve'), may hold values from 0.02 to 20
- courant: float32 [72, 8192], P(None, 'curve'), may hold values from 0.05 to 0.9
- cloud_levels: int32 [8192], P('curve'), may hold values from 1 to 72
- neighbors: int32 [4, 256], P(None, 'curve'), may hold values from 0 to 255, as said below
Outputs:
- span_state: float32 [72, 48, 8192], P(None, 'field', 'curve')
- dynamics_state: float32 [72, 48, 4096], P(None, 'field', 'curve')
Inputs may be any that keep to these rules, and one draw needn't show every extreme that they name: `span_of`: from the columns of one block at most 2 go to one span; in every draw one span receives exactly 2 columns from every block. `neighbors`: edges pair up: if element f lies across edge s of element g, then g lies across edge (s + 2) % 4 of f. Every neighbour lies in the same block of 4 elements as the element, or in the block just before or just after it along the curve, the last block being followed by the first.
All inputs are finite; a program needn't handle non-finite values.
Results may differ from a plain program's by a relative error of at most 0.00007.
Values sent between devices are 32-bit elements; how exact they have to be, the bound alone decides.
No kernel may reach another device: no remote copies, remote signals or barrier semaphores. Data moves between devices by JAX's collectives and lax.ppermute only.
A program may use at most 128 MiB of HBM per device.

v0:
```python
import jax
import jax.numpy as jnp
import numpy as np
from jax import lax
from jax.sharding import PartitionSpec as P

viscosity = 0.02
edge_table = np.array([[0, 1, 2, 3], [3, 7, 11, 15], [15, 14, 13, 12], [12, 8, 4, 0]])
opposite = np.array([2, 3, 0, 1])
scatter_table = (np.arange(16)[:, None, None] == edge_table[None, :, :]).astype(np.float32)
second_diff = np.array(
    [[-1.0, 1.0, 0.0, 0.0], [1.0, -2.0, 1.0, 0.0], [0.0, 1.0, -2.0, 1.0], [0.0, 0.0, 1.0, -1.0]]
)
lap_table = np.kron(np.eye(4), second_diff) + np.kron(second_diff, np.eye(4))


def extended_2(block, sides, width):
    for axis, dim in sides:
        count = lax.axis_size(axis)
        forward = [(i, i + 1) for i in range(count - 1)]
        forward.append((count - 1, 0))
        backward = [(target, source) for source, target in forward]
        low = lax.ppermute(
            lax.slice_in_dim(block, block.shape[dim] - width, None, axis=dim), axis, forward
        )
        high = lax.ppermute(lax.slice_in_dim(block, 0, width, axis=dim), axis, backward)
        block = jnp.concatenate([low, block, high], axis=dim)
    return block


def level_factors(coefficients):
    levels = coefficients.shape[0]
    coef_above = jnp.zeros_like(coefficients[0])
    ratio_above = jnp.zeros_like(coefficients[0])
    inverses = []
    ratios = []
    aboves = []
    for level in range(levels):
        coef_here = coefficients[level]
        inverse = 1.0 / (1.0 + coef_above + coef_here - coef_above * ratio_above)
        ratio_here = coef_here * inverse
        inverses.append(inverse)
        ratios.append(ratio_here)
        aboves.append(coef_above)
        coef_above = coef_here
        ratio_above = ratio_here
    return (jnp.stack(inverses), jnp.stack(ratios), jnp.stack(aboves))


def column_physics(column_state, fall_cols, cloud_cols, factors):
    inverse, sweep_ratio, coef_above = factors
    levels = column_state.shape[0]
    active = jnp.arange(levels, dtype=jnp.int32)[:, None] >= (levels - cloud_cols)[None, :]
    fall_rate = jnp.where(active, fall_cols, jnp.zeros_like(fall_cols))
    fall_flux = fall_rate[:, None, :] * column_state
    from_above = jnp.concatenate([jnp.zeros_like(fall_flux[:1]), fall_flux[:-1]], axis=0)
    settled = column_state - fall_flux + from_above
    partial_sol = jnp.zeros_like(settled[0])
    partials = []
    for level in range(levels):
        partial_sol = (settled[level] + coef_above[level][None, :] * partial_sol) * inverse[level][
            None, :
        ]
        partials.append(partial_sol)
    solved = jnp.zeros_like(settled[0])
    solution = [None] * levels
    for level in range(levels - 1, -1, -1):
        solved = partials[level] + sweep_ratio[level][None, :] * solved
        solution[level] = solved
    return jnp.stack(solution)


def routing(span_of, spans, capacity):
    columns = span_of.shape[0]
    onehot = (span_of[:, None] == jnp.arange(spans, dtype=jnp.int32)[None, :]).astype(jnp.int32)
    order_rank = jnp.sum(jnp.cumsum(onehot, axis=0) * onehot, axis=1) - 1
    slot_index = span_of * capacity + order_rank
    source = jnp.zeros((spans * capacity,), jnp.int32) + columns
    source = source.at[slot_index].set(jnp.arange(columns, dtype=jnp.int32))
    return (slot_index, source)


def pack_slots(values, source):
    padded = jnp.concatenate([values, jnp.zeros_like(values[..., :1])], axis=-1)
    return jnp.take(padded, source, axis=-1)


def edge_sum(field, halo_index):
    levels, fields, columns = field.shape
    elements = columns // 16
    arranged = field.reshape(levels, fields, 16, elements)
    edge_vals = arranged[:, :, edge_table, :]
    extended = extended_2(edge_vals, (("curve", 4),), elements)
    facing = extended[:, :, opposite, ::-1, :]
    pieces = []
    for side in range(4):
        pieces.append(jnp.take(facing[:, :, side], halo_index[side], axis=-1))
    across = jnp.stack(pieces, axis=2)
    change = 0.5 * (across - edge_vals)
    increment = jnp.einsum(
        "nsp,lfspe->lfne",
        jnp.asarray(scatter_table, dtype=field.dtype),
        change,
        precision=lax.Precision.HIGHEST,
    )
    return (arranged + increment).reshape(levels, fields, columns)


def apply_lap(field):
    levels, fields, columns = field.shape
    arranged = field.reshape(levels, fields, 16, columns // 16)
    result = jnp.einsum(
        "nm,lfme->lfne",
        jnp.asarray(lap_table, dtype=field.dtype),
        arranged,
        precision=lax.Precision.HIGHEST,
    )
    return result.reshape(levels, fields, columns)


def per_device(column_state, span_of, diffusivity, courant, cloud_levels, neighbors):
    spans = lax.axis_size("curve")
    columns = column_state.shape[2]
    capacity = 2 * columns // spans
    slot_index, source = routing(span_of, spans, capacity)
    factors = level_factors(diffusivity)
    updated = column_physics(
        lax.all_to_all(
            pack_slots(column_state, source), "curve", split_axis=2, concat_axis=2, tiled=True
        ),
        courant,
        cloud_levels,
        factors,
    )
    returned = lax.all_to_all(updated, "curve", split_axis=2, concat_axis=2, tiled=True)
    physics_state = jnp.take(returned, slot_index, axis=-1)
    elements = columns // 16
    device = lax.axis_index("curve")
    owner_block = neighbors // elements
    offset = jnp.mod(owner_block - device + 1, spans)
    halo_index = offset * elements + jnp.mod(neighbors, elements)
    smoothed = edge_sum(physics_state, halo_index)
    second = edge_sum(apply_lap(smoothed), halo_index)
    dynamics_state = smoothed - viscosity * apply_lap(second)
    return (updated, dynamics_state)


def solution(mesh):
    placed = (
        P(None, "field", "curve"),
        P("curve"),
        P(None, "curve"),
        P(None, "curve"),
        P("curve"),
        P(None, "curve"),
    )
    return jax.shard_map(
        per_device,
        mesh=mesh,
        in_specs=placed,
        out_specs=(P(None, "field", "curve"), P(None, "field", "curve")),
        check_vma=False,
    )
```

profile of v0, /device:TPU:16, one launch (start us, length us, event | category | flops | bytes accessed | tf_op | source)
XLA Modules:
  0.0 114.3 jit_solution(11588912253359988965)
XLA Ops:
  0.6 0.7 fusion.9
  1.5 0.8 select_reduce_fusion
  2.3 0.7 compare_and_fusion.4
  3.0 0.8 scatter_custom_fusion
  3.8 1.2 %copy.6529 = f32[72,12,64]{0,1,2:T(8,128)S(1)} copy(f32[72,12,64]{0,2,1:T(8,128)} %param.18) | data formatting | bytes 442368 | tf_op args[0]
  5.1 0.8 gather_fusion
  6.1 1.9 %reshape.36257 = f32[64,1,1728]{2,1,0:T(1,128)} reshape(f32[128,12,72]{2,1,0:T(8,128)S(1)} %fusion.253) | data formatting | bytes 884736
  8.0 11.9 %all-to-all-start = ((f32[64,1,1728]{2,1,0:T(1,128)}), f32[64,1,1728]{2,1,0:T(1,128)S(1)}, u32[]{:S(2)}, u32[]{:S(2)}) async-start(f32[64,1,1728]{2,1,0:T(1,128)} %reshape.36257), calls=%async_computation | async-start | bytes 917504 | tf_op jit(solution)/shard_map/all_to_all | solution.py:128
  20.9 0.7 fusion.144
  21.7 14.1 %all-to-all-done = f32[64,1,1728]{2,1,0:T(1,128)S(1)} async-done(((f32[64,1,1728]{2,1,0:T(1,128)}), f32[64,1,1728]{2,1,0:T(1,128)S(1)}, u32[]{:S(2)}, u32[]{:S(2)}) %all-to-all-start) | async-done | bytes 442400 | tf_op jit(solution)/shard_map/all_to_all | solution.py:128
  35.7 0.5 broadcast.31037
  36.3 1.7 %reduce = f32[64,1728]{1,0:T(8,128)S(1)} reduce(f32[64,1,1728]{2,1,0:T(1,128)S(1)} %all-to-all-done, f32[]{:T(128)} %broadcast.31037), dimensions={1}, to_apply=%all_to_all.6.reduce_sub_computation | reduce | bytes 884740 | tf_op jit(solution)/shard_map/all_to_all | solution.py:128
  38.0 0.9 reshape.36258
  41.8 1.0 multiply_add_fusion.36
  42.8 0.7 stack.136
  43.6 0.5 copy.6718
  44.1 1.9 %reshape.36259 = f32[64,1,1728]{2,1,0:T(1,128)} reshape(f32[128,12,72]{2,1,0:T(8,128)S(1)} %bitcast.1841) | data formatting | bytes 884736
  46.0 6.6 %all-to-all-start.1 = ((f32[64,1,1728]{2,1,0:T(1,128)}), f32[64,1,1728]{2,1,0:T(1,128)S(1)}, u32[]{:S(2)}, u32[]{:S(2)}) async-start(f32[64,1,1728]{2,1,0:T(1,128)} %reshape.36259), calls=%async_computation.1 | async-start | bytes 917504 | tf_op jit(solution)/shard_map/all_to_all | solution.py:135
  52.7 0.6 compare_and_fusion.3
  53.3 15.1 %all-to-all-done.1 = f32[64,1,1728]{2,1,0:T(1,128)S(1)} async-done(((f32[64,1,1728]{2,1,0:T(1,128)}), f32[64,1,1728]{2,1,0:T(1,128)S(1)}, u32[]{:S(2)}, u32[]{:S(2)}) %all-to-all-start.1) | async-done | bytes 442400 | tf_op jit(solution)/shard_map/all_to_all | solution.py:135
  68.4 1.7 %reduce.1 = f32[64,1728]{1,0:T(8,128)S(1)} reduce(f32[64,1,1728]{2,1,0:T(1,128)S(1)} %all-to-all-done.1, f32[]{:T(128)} %broadcast.31037), dimensions={1}, to_apply=%all_to_all.7.reduce_sub_computation | reduce | bytes 884740 | tf_op jit(solution)/shard_map/all_to_all | solution.py:135
  70.1 0.9 reshape.36260
  71.0 0.6 gather_fusion.1
  72.0 0.7 copy-done
  72.9 0.8 gather_fusion.2
  73.8 1.8 %collective-permute-start.1 = (f32[72,12,4,4,4]{0,4,3,2,1:T(4,128)S(1)}, f32[72,12,4,4,4]{0,4,3,2,1:T(4,128)S(1)}, u32[]{:S(2)}, u32[]{:S(2)}) collective-permute-start(f32[72,12,4,4,4]{0,4,3,2,1:T(4,128)S(1)} %bitcast.1849), channel_id=1, source_target_pairs={{4,0},{8,4},{12,8},{16,12},{20,16},{24,20},{28,24},{32,28},{36,32}... | collective-permute-start | bytes 663560 | tf_op jit(solution)/shard_map/ppermute | solution.py:26
  75.6 0.6 pad_clamp_fusion.1
  76.2 0.6 pad_clamp_fusion.2
  76.8 4.1 %collective-permute-done.1 = f32[72,12,4,4,4]{0,4,3,2,1:T(4,128)S(1)} collective-permute-done((f32[72,12,4,4,4]{0,4,3,2,1:T(4,128)S(1)}, f32[72,12,4,4,4]{0,4,3,2,1:T(4,128)S(1)}, u32[]{:S(2)}, u32[]{:S(2)}) %collective-permute-start.1) | collective-permute-done | bytes 221216 | tf_op jit(solution)/shard_map/ppermute | solution.py:26
  80.9 5.2 %collective-permute-done = f32[72,12,4,4,4]{0,4,3,2,1:T(4,128)S(1)} collective-permute-done((f32[72,12,4,4,4]{0,4,3,2,1:T(4,128)S(1)}, f32[72,12,4,4,4]{0,4,3,2,1:T(4,128)S(1)}, u32[]{:S(2)}, u32[]{:S(2)}) %collective-permute-start) | collective-permute-done | bytes 221216 | tf_op jit(solution)/shard_map/ppermute | solution.py:23
  86.5 0.6 gather_fusion.3
  87.6 0.6 gather_fusion.6
  88.6 0.6 gather_fusion.9
  89.7 0.7 gather_fusion.8
  90.8 0.7 gather_fusion.7
  91.9 0.6 copy-done.1
  92.5 0.7 fusion.2
  94.1 0.8 gather_fusion.4
  95.2 0.5 collective-permute-start.2
  95.7 4.8 %collective-permute-done.3 = f32[72,12,4,4,4]{0,4,3,2,1:T(4,128)S(1)} collective-permute-done((f32[72,12,4,4,4]{0,4,3,2,1:T(4,128)S(1)}, f32[72,12,4,4,4]{0,4,3,2,1:T(4,128)S(1)}, u32[]{:S(2)}, u32[]{:S(2)}) %collective-permute-start.3) | collective-permute-done | bytes 221216 | tf_op jit(solution)/shard_map/ppermute | solution.py:26
  100.5 5.5 %collective-permute-done.2 = f32[72,12,4,4,4]{0,4,3,2,1:T(4,128)S(1)} collective-permute-done((f32[72,12,4,4,4]{0,4,3,2,1:T(4,128)S(1)}, f32[72,12,4,4,4]{0,4,3,2,1:T(4,128)S(1)}, u32[]{:S(2)}, u32[]{:S(2)}) %collective-permute-start.2) | collective-permute-done | bytes 221216 | tf_op jit(solution)/shard_map/ppermute | solution.py:23
  106.4 0.6 gather_fusion.5
  107.4 0.7 gather_fusion.10
  108.4 0.7 gather_fusion.13
  109.4 0.7 gather_fusion.12
  110.6 0.9 gather_fusion.11
  112.2 0.7 fusion.3
  113.4 0.9 copy.6743
  (209 shorter events, 10.1 us)
Async XLA Ops:
  6.1 14.0 %copy-start.24 = (s32[4]{0:T(128)S(1)}, s32[4]{0:T(128)}, u32[]{:S(2)}) copy-start(s32[4]{0:T(128)} %constant.165) | copy-start | bytes 52
  6.1 14.2 %copy-start.7 = (f32[72,128]{1,0:T(8,128)S(1)}, f32[72,128]{1,0:T(8,128)}, u32[]{:S(2)}) copy-start(f32[72,128]{1,0:T(8,128)} %param.20) | copy-start | bytes 110596
  6.1 14.8 %copy-start.25 = (s32[128]{0:T(128)S(1)}, s32[128]{0:T(128)}, u32[]{:S(2)}) copy-start(s32[128]{0:T(128)} %param.22) | copy-start | bytes 1540
  6.1 15.5 %copy-start.8 = (f32[72,128]{1,0:T(8,128)S(1)}, f32[72,128]{1,0:T(8,128)}, u32[]{:S(2)}) copy-start(f32[72,128]{1,0:T(8,128)} %param.21) | copy-start | bytes 110596
  8.0 27.7 %all-to-all-start = ((f32[64,1,1728]{2,1,0:T(1,128)}), f32[64,1,1728]{2,1,0:T(1,128)S(1)}, u32[]{:S(2)}, u32[]{:S(2)}) async-start(f32[64,1,1728]{2,1,0:T(1,128)} %reshape.36257), calls=%async_computation | async-start | bytes 917504 | tf_op jit(solution)/shard_map/all_to_all | solution.py:128
  43.6 2.4 %copy-start.6 = (f32[72,12,128]{2,0,1:T(8,128)}, f32[72,12,128]{2,0,1:T(8,128)S(1)}, u32[]{:S(2)}) copy-start(f32[72,12,128]{2,0,1:T(8,128)S(1)} %stack.136) | copy-start | bytes 1327108
  44.1 8.5 %copy-start.22 = (s32[4,4]{1,0:T(4,128)S(1)}, s32[4,4]{1,0:T(4,128)}, u32[]{:S(2)}) copy-start(s32[4,4]{1,0:T(4,128)} %param.23) | copy-start | bytes 196
  44.1 9.2 %copy-start.23 = (s32[16]{0:T(128)S(1)}, s32[16]{0:T(128)}, u32[]{:S(2)}) copy-start(s32[16]{0:T(128)} %constant.163) | copy-start | bytes 196
  46.0 22.4 %all-to-all-start.1 = ((f32[64,1,1728]{2,1,0:T(1,128)}), f32[64,1,1728]{2,1,0:T(1,128)S(1)}, u32[]{:S(2)}, u32[]{:S(2)}) async-start(f32[64,1,1728]{2,1,0:T(1,128)} %reshape.36259), calls=%async_computation.1 | async-start | bytes 917504 | tf_op jit(solution)/shard_map/all_to_all | solution.py:135
  53.3 34.3 %copy-start.13 = (s32[1024]{0:T(1024)}, s32[1024]{0:T(1024)S(1)}, u32[]{:S(2)}) copy-start(s32[1024]{0:T(1024)S(1)} %pad_clamp_fusion.3) | copy-start | bytes 12292
  53.3 35.3 %copy-start.12 = (s32[1024]{0:T(1024)}, s32[1024]{0:T(1024)S(1)}, u32[]{:S(2)}) copy-start(s32[1024]{0:T(1024)S(1)} %pad_clamp_fusion) | copy-start | bytes 12292
  71.9 0.7 copy-start
  73.8 7.1 %collective-permute-start.1 = (f32[72,12,4,4,4]{0,4,3,2,1:T(4,128)S(1)}, f32[72,12,4,4,4]{0,4,3,2,1:T(4,128)S(1)}, u32[]{:S(2)}, u32[]{:S(2)}) collective-permute-start(f32[72,12,4,4,4]{0,4,3,2,1:T(4,128)S(1)} %bitcast.1849), channel_id=1, source_target_pairs={{4,0},{8,4},{12,8},{16,12},{20,16},{24,20},{28,24},{32,28},{36,32}... | collective-permute-start | bytes 663560 | tf_op jit(solution)/shard_map/ppermute | solution.py:26
  75.6 10.5 %collective-permute-start = (f32[72,12,4,4,4]{0,4,3,2,1:T(4,128)S(1)}, f32[72,12,4,4,4]{0,4,3,2,1:T(4,128)S(1)}, u32[]{:S(2)}, u32[]{:S(2)}) collective-permute-start(f32[72,12,4,4,4]{0,4,3,2,1:T(4,128)S(1)} %bitcast.1850), channel_id=1, source_target_pairs={{0,4},{4,8},{8,12},{12,16},{16,20},{20,24},{24,28},{28,32},{32,36}... | collective-permute-start | bytes 663560 | tf_op jit(solution)/shard_map/ppermute | solution.py:23
  87.6 0.7 copy-start.14
  88.6 0.6 copy-start.18
  89.6 0.8 copy-start.20
  90.8 0.8 copy-start.16
  91.5 1.0 copy-start.1
  91.6 1.0 copy-start.10
  91.6 1.7 %copy-start.9 = (f32[16,16,1,1]{1,0,3,2:T(8,128)S(1)}, f32[16,16,1,1]{1,0,3,2:T(8,128)}, u32[]{:S(2)}) copy-start(f32[16,16,1,1]{1,0,3,2:T(8,128)} %constant.170) | copy-start | bytes 3076
  93.2 0.7 copy-start.2
  95.1 10.9 %copy-start.4 = (f32[16,72,12,4]{1,3,0,2:T(4,128)}, f32[16,72,12,4]{1,3,0,2:T(4,128)S(1)}, u32[]{:S(2)}) copy-start(f32[16,72,12,4]{1,3,0,2:T(4,128)S(1)} %copy.6733) | copy-start | bytes 663556
  95.1 5.4 %collective-permute-start.3 = (f32[72,12,4,4,4]{0,4,3,2,1:T(4,128)S(1)}, f32[72,12,4,4,4]{0,4,3,2,1:T(4,128)S(1)}, u32[]{:S(2)}, u32[]{:S(2)}) collective-permute-start(f32[72,12,4,4,4]{0,4,3,2,1:T(4,128)S(1)} %bitcast.1842), channel_id=1, source_target_pairs={{4,0},{8,4},{12,8},{16,12},{20,16},{24,20},{28,24},{32,28},{36,32}... | collective-permute-start | bytes 663560 | tf_op jit(solution)/shard_map/ppermute | solution.py:26
  95.2 10.8 %collective-permute-start.2 = (f32[72,12,4,4,4]{0,4,3,2,1:T(4,128)S(1)}, f32[72,12,4,4,4]{0,4,3,2,1:T(4,128)S(1)}, u32[]{:S(2)}, u32[]{:S(2)}) collective-permute-start(f32[72,12,4,4,4]{0,4,3,2,1:T(4,128)S(1)} %bitcast.1843), channel_id=1, source_target_pairs={{0,4},{4,8},{8,12},{12,16},{16,20},{20,24},{24,28},{28,32},{32,36}... | collective-permute-start | bytes 663560 | tf_op jit(solution)/shard_map/ppermute | solution.py:23
  109.4 0.8 copy-start.19
  109.4 0.8 copy-start.21
  110.6 0.9 copy-start.15
  110.6 0.9 copy-start.17
  110.6 1.1 copy-start.5
  111.5 0.7 copy-start.11
  111.5 1.4 %copy-start.3 = (f32[72,12,16,4]{0,2,3,1:T(8,128)S(1)}, f32[72,12,16,4]{0,2,3,1:T(8,128)}, u32[]{:S(2)}) copy-start(f32[72,12,16,4]{0,2,3,1:T(8,128)} %copy-done.2) | copy-start | bytes 663556
where the time goes:
time: 115 us; the launch traced here: 114 us
  waiting for transfers between devices  48.8 us (42%)
  local copies, waits for them, and re-layouts  26.8 us (23%)
  starting transfers between devices  20.9 us (18%)
  other arithmetic  13.3 us (12%)
  matrix products  2.25 us (2%)
  between operations  2.19 us (2%)
    all_to_all x1, waiting for transfers between devices, per_device(): lax.all_to_all(updated, 'curve', split_axis=2, concat_axis=2, tiled=True)  15.1 us
    all_to_all x1, waiting for transfers between devices, per_device(): lax.all_to_all(pack_slots(column_state, source), 'curve', split_axis=2, c...  14.1 us
    all_to_all x1, starting transfers between devices, per_device(): lax.all_to_all(pack_slots(column_state, source), 'curve', split_axis=2, c...  11.9 us
    ppermute x2, waiting for transfers between devices, extended_2(): lax.ppermute(lax.slice_in_dim(block, block.shape[dim] - width, None, axis...  10.8 us
    unnamed x57, local copies, waits for them, and re-layouts  8.96 us
    ppermute x2, waiting for transfers between devices, extended_2(): lax.ppermute(lax.slice_in_dim(block, 0, width, axis=dim), axis, backward)  8.9 us
    all_to_all x1, starting transfers between devices, per_device(): lax.all_to_all(updated, 'curve', split_axis=2, concat_axis=2, tiled=True)  6.59 us
    gather x8, local copies, waits for them, and re-layouts, edge_sum(): pieces.append(jnp.take(facing[:, :, side], halo_index[side], axis=-1))  5.79 us
  transfers between devices with their start and end apart: 6, of which 6 were waited for; matrix products, arithmetic and copies ran while one was open for 3% of the time, Pallas kernels for 0%

commit v1 on v0

v1 whole, which is shorter than its diff:
```python
import numpy as np
import jax
import jax.numpy as jnp
from jax import lax
from jax.experimental import pallas as pl
from jax.experimental.pallas import tpu as pltpu
from jax.sharding import PartitionSpec as P

LEV = 72
HALF = LEV // 2
NF = 12
PAIR = NF // 2
COL = 64
SLOT = 128
WORDS = 1024
CHUNKS = WORDS // 128
STATE = NF * LEV
SPANS = 64
viscosity = 0.02

second_diff = np.array(
    [[-1.0, 1.0, 0.0, 0.0], [1.0, -2.0, 1.0, 0.0], [0.0, 1.0, -2.0, 1.0], [0.0, 0.0, 1.0, -1.0]]
)
lap_nodes = np.kron(np.eye(4), second_diff) + np.kron(second_diff, np.eye(4))
lap_columns = np.kron(lap_nodes, np.eye(4)).astype(np.float32)

f32 = jnp.float32
bf16 = jnp.bfloat16


def iota(shape, axis):
    return lax.broadcasted_iota(jnp.int32, shape, axis)


def split3(x):
    hi = x.astype(bf16)
    rest = x - hi.astype(f32)
    mid = rest.astype(bf16)
    lo = (rest - mid.astype(f32)).astype(bf16)
    return hi, mid, lo


def split2(x):
    hi = x.astype(bf16)
    return hi, (x - hi.astype(f32)).astype(bf16)


def dot(a, b):
    return jnp.dot(a, b, preferred_element_type=f32)


def slots_of(span_row):
    row = span_row.astype(f32)
    square = jnp.broadcast_to(row, (COL, COL))
    column = jnp.sum(
        jnp.where(iota((COL, COL), 0) == iota((COL, COL), 1), square, 0.0), axis=1, keepdims=True
    )
    earlier = jnp.logical_and(column == square, iota((COL, COL), 0) < iota((COL, COL), 1))
    rank = jnp.sum(jnp.where(earlier, 1.0, 0.0), axis=0, keepdims=True)
    return (2.0 * row + rank).astype(jnp.int32)


def active_rate(courant, cloud_row):
    level = iota((LEV, SLOT), 0)
    return jnp.where(level >= LEV - cloud_row, courant, 0.0)


def pack_kernel(x_ref, span_ref, diff_ref, courant_ref, cloud_ref, near_ref, out_ref, slot_ref):
    slot_row = slots_of(span_ref[...])
    slot_ref[...] = jnp.broadcast_to(jnp.concatenate([slot_row, slot_row], axis=1), (8, SLOT))
    pick = (iota((SLOT, COL), 0) == slot_row).astype(f32).astype(bf16)
    state = jnp.concatenate([x_ref[f] for f in range(NF)], axis=1)
    hi, mid, lo = split3(state)
    packed = dot(pick, hi) + dot(pick, mid) + dot(pick, lo)
    diff_t = diff_ref[...].T
    rate_t = active_rate(courant_ref[...], cloud_ref[...]).T
    near = near_ref[...].astype(f32)
    near_row = jnp.concatenate([near[s : s + 1, :] for s in range(4)], axis=1)
    near_t = jnp.broadcast_to(near_row, (SLOT, 16))
    message = jnp.concatenate([packed, diff_t, rate_t, near_t], axis=1)
    for k in range(CHUNKS):
        out_ref[pl.ds(k, SLOT, stride=CHUNKS), :] = message[:, 128 * k : 128 * k + 128]


def turn_kernel(x_ref, out_ref):
    for f in range(PAIR):
        both = jnp.concatenate([x_ref[f], x_ref[f + PAIR]], axis=0)
        out_ref[pl.ds(f * LEV, LEV), :] = both.T


def chunk_t(recv_ref, k):
    return recv_ref[pl.ds(k, SLOT, stride=CHUNKS), :].T


def solve(coef_ref, rate_ref, groups, part_ref, ratio_ref):
    rows = (PAIR, 128)
    zero = jnp.zeros(rows, f32)

    def row(ref, k):
        return jnp.broadcast_to(ref[pl.ds(k, 1), :], rows)

    count = len(groups)
    top_ratio, bot_ratio = zero, zero
    top_part, bot_part = [zero] * count, [zero] * count
    top_flux = [zero] * count
    top_above = zero
    bot_below = row(coef_ref, LEV - 1)
    last = row(rate_ref, LEV - 1)
    bot_state = [load(LEV - 1) for load, _ in groups]
    bot_flux = [last * x for x in bot_state]
    for i in range(HALF):
        t, u = i, LEV - 1 - i
        top_next = row(coef_ref, t)
        bot_next = row(coef_ref, u - 1)
        top_inv = 1.0 / (1.0 + top_above + top_next - top_above * top_ratio)
        bot_inv = 1.0 / (1.0 + bot_below + bot_next - bot_below * bot_ratio)
        top_ratio = top_next * top_inv
        bot_ratio = bot_next * bot_inv
        ratio_ref[i] = top_ratio
        ratio_ref[HALF + i] = bot_ratio
        top_rate = row(rate_ref, t)
        above_rate = row(rate_ref, u - 1)
        for g, (load, _) in enumerate(groups):
            x = load(t)
            flux = top_rate * x
            settled = x - flux + top_flux[g]
            top_flux[g] = flux
            top_part[g] = (settled + top_above * top_part[g]) * top_inv
            part_ref[g, i] = top_part[g]
            above = load(u - 1)
            above_flux = above_rate * above
            settled = bot_state[g] - bot_flux[g] + above_flux
            bot_state[g] = above
            bot_flux[g] = above_flux
            bot_part[g] = (settled + bot_below * bot_part[g]) * bot_inv
            part_ref[g, HALF + i] = bot_part[g]
        top_above = top_next
        bot_below = bot_next
    meet = 1.0 / (1.0 - top_ratio * bot_ratio)
    top, bot = [], []
    for g, (_, store) in enumerate(groups):
        top.append((top_part[g] + top_ratio * bot_part[g]) * meet)
        bot.append((bot_part[g] + bot_ratio * top_part[g]) * meet)
        store(HALF - 1, top[g])
        store(HALF, bot[g])
    for i in range(HALF - 2, -1, -1):
        top_ratio = ratio_ref[i]
        bot_ratio = ratio_ref[HALF + i]
        for g, (_, store) in enumerate(groups):
            top[g] = part_ref[g, i] + top_ratio * top[g]
            bot[g] = part_ref[g, HALF + i] + bot_ratio * bot[g]
            store(i, top[g])
            store(LEV - 1 - i, bot[g])


def strided(in_ref, out_ref, base):
    def load(level):
        return in_ref[pl.ds(base + level, PAIR, stride=LEV), :]

    def store(level, value):
        out_ref[pl.ds(base + level, PAIR, stride=LEV), :] = value

    return load, store


def element_kernel(recv_ref, slot_ref, x_ref, out_ref, coef_ref, rate_ref, part_ref, ratio_ref):
    spread = (iota((SLOT, 128), 0) == slot_ref[0:1, :]).astype(f32).astype(bf16)
    tail = jnp.concatenate([chunk_t(recv_ref, CHUNKS - 2), chunk_t(recv_ref, CHUNKS - 1)], axis=0)
    begin = STATE - 128 * (CHUNKS - 2)
    hi, mid, lo = split3(tail[begin : begin + 2 * LEV])
    columns = dot(hi, spread) + dot(mid, spread) + dot(lo, spread)
    coef_ref[...] = columns[:LEV]
    rate_ref[...] = columns[LEV:]
    solve(coef_ref, rate_ref, [strided(x_ref, out_ref, 0)], part_ref, ratio_ref)


def halo_matrix(recv_ref, lap_ref, matrix_ref):
    device = lax.axis_index("curve")
    lap = lap_ref[...].astype(bf16)
    lane = iota((1, COL), 1)
    node = lane // 4
    node_row, node_col = node // 4, node % 4
    on_edge = [node_row == 0, node_col == 3, node_row == 3, node_col == 0]
    facing = [node + 12, node - 3, node - 12, node + 3]
    edges = sum(jnp.where(edge, 1.0, 0.0) for edge in on_edge)
    word = iota((128, 4 * COL), 0) - (128 - 16)
    place = iota((128, 4 * COL), 1)
    spread = (word == (place // COL) * 4 + place % 4).astype(f32).astype(bf16)
    rows = []
    for o in range(3):
        block = lax.rem(device + (o - 1) + SPANS, SPANS)
        rows.append(recv_ref[pl.ds(block * 16 + CHUNKS - 1, 1), :])
    rows = jnp.concatenate(rows + [jnp.zeros((5, 128), f32)], axis=0)
    near = dot(rows.astype(bf16), spread).astype(jnp.int32)
    source = iota((5 * COL, COL), 0)
    sums = []
    for o in range(3):
        own = source == lane + (o + 1) * COL
        total = jnp.where(own, 1.0 - 0.5 * edges, 0.0)
        for s in range(4):
            element = near[o : o + 1, s * COL : (s + 1) * COL]
            relative = lax.rem(element // 4 - device + (2 + SPANS), SPANS)
            target = relative * COL + facing[s] * 4 + element % 4
            target = jnp.where(on_edge[s], target, -1)
            total = total + jnp.where(source == target, 0.5, 0.0)
        sums.append(total)
    second = dot(sums[1][COL : 4 * COL].astype(bf16), lap).astype(bf16)
    matrix = jnp.zeros((5 * COL, COL), f32)
    for o in range(3):
        inner = dot(lap, second[o * COL : (o + 1) * COL]).astype(bf16)
        matrix = matrix + dot(sums[o].astype(bf16), inner)
    matrix = sums[1] - viscosity * matrix
    zero = jnp.zeros((COL, COL), f32)
    for o in range(5):
        block = matrix[o * COL : (o + 1) * COL]
        matrix_ref[o] = jnp.concatenate(
            [jnp.concatenate([block, zero], axis=1), jnp.concatenate([zero, block], axis=1)], axis=0
        )


def span_kernel(
    recv_ref, diff_ref, courant_ref, cloud_ref, lap_ref, out_ref, matrix_ref,
    state_ref, rate_ref, part_ref, ratio_ref,
):
    halo_matrix(recv_ref, lap_ref, matrix_ref)
    rate_ref[...] = active_rate(courant_ref[...], cloud_ref[...])
    for k in range(CHUNKS - 1):
        state_ref[pl.ds(128 * k, 128), :] = chunk_t(recv_ref, k)
    groups = [strided(state_ref, out_ref, g * PAIR * LEV) for g in range(2)]
    solve(diff_ref, rate_ref, groups, part_ref, ratio_ref)


def dynamics_kernel(a_ref, b_ref, c_ref, d_ref, e_ref, matrix_ref, out_ref):
    total = jnp.zeros((PAIR * LEV, 128), f32)
    for o, ref in enumerate((a_ref, b_ref, c_ref, d_ref, e_ref)):
        x_hi, x_lo = split2(ref[...])
        m_hi, m_lo = split2(matrix_ref[o])
        total = total + (dot(x_hi, m_hi) + dot(x_lo, m_hi) + dot(x_hi, m_lo))
    for f in range(PAIR):
        turned = total[f * LEV : (f + 1) * LEV].T
        out_ref[f] = turned[:COL]
        out_ref[f + PAIR] = turned[COL:]


def per_device(column_state, span_of, diffusivity, courant, cloud_levels, neighbors):
    shape = jax.ShapeDtypeStruct
    params = pltpu.CompilerParams(vmem_limit_bytes=32 * 1024 * 1024)
    x = jnp.transpose(column_state, (1, 2, 0))
    span_row = span_of.reshape(1, COL)
    cloud_row = cloud_levels.reshape(1, SLOT)
    message, slots = pl.pallas_call(
        pack_kernel,
        out_shape=(shape((SLOT * CHUNKS, 128), f32), shape((8, SLOT), jnp.int32)),
        compiler_params=params,
        name="pack",
    )(x, span_row, diffusivity, courant, cloud_row, neighbors)
    turned = pl.pallas_call(
        turn_kernel,
        out_shape=shape((PAIR * LEV, 128), f32),
        compiler_params=params,
        name="turn",
    )(x)
    received = lax.all_to_all(
        message.reshape(SPANS, 16, 128), "curve", split_axis=0, concat_axis=0, tiled=True
    ).reshape(SLOT * CHUNKS, 128)
    physics = pl.pallas_call(
        element_kernel,
        out_shape=shape((PAIR * LEV, 128), f32),
        scratch_shapes=[
            pltpu.VMEM((LEV, 128), f32),
            pltpu.VMEM((LEV, 128), f32),
            pltpu.VMEM((1, LEV, PAIR, 128), f32),
            pltpu.VMEM((LEV, PAIR, 128), f32),
        ],
        compiler_params=params,
        name="element",
    )(received, slots, turned)
    halo = {}
    for k in (2, 1, -1, -2):
        halo[k] = lax.ppermute(physics, "curve", [(i, (i + k) % SPANS) for i in range(SPANS)])
    span_state, matrix = pl.pallas_call(
        span_kernel,
        out_shape=(shape((STATE, SLOT), f32), shape((5, 128, 128), f32)),
        scratch_shapes=[
            pltpu.VMEM(((CHUNKS - 1) * 128, 128), f32),
            pltpu.VMEM((LEV, 128), f32),
            pltpu.VMEM((2, LEV, PAIR, 128), f32),
            pltpu.VMEM((LEV, PAIR, 128), f32),
        ],
        compiler_params=params,
        name="span",
    )(received, diffusivity, courant, cloud_row, jnp.asarray(lap_columns))
    dynamics = pl.pallas_call(
        dynamics_kernel,
        out_shape=shape((NF, COL, LEV), f32),
        compiler_params=params,
        name="dynamics",
    )(halo[2], halo[1], physics, halo[-1], halo[-2], matrix)
    return (
        jnp.transpose(span_state.reshape(NF, LEV, SLOT), (1, 0, 2)),
        jnp.transpose(dynamics, (2, 0, 1)),
    )


def solution(mesh):
    placed = (
        P(None, "field", "curve"),
        P("curve"),
        P(None, "curve"),
        P(None, "curve"),
        P("curve"),
        P(None, "curve"),
    )
    return jax.shard_map(
        per_device,
        mesh=mesh,
        in_specs=placed,
        out_specs=(P(None, "field", "curve"), P(None, "field", "curve")),
        check_vma=False,
    )
```

time: 115 us -> 51.6 us (0.45)
  waiting for transfers between devices: 48.8 us -> 22.6 us
  local copies, waits for them, and re-layouts: 26.8 us -> 3.21 us
  other arithmetic: 13.3 us -> 0 us
  Pallas kernels: 0 us -> 5.5 us
  matrix products: 2.25 us -> 0 us
  starting transfers between devices: 20.9 us -> 19.2 us
  between operations: 2.19 us -> 0.7 us
    ppermute x4, waiting for transfers between devices: 19.7 us -> 5.54 us  [per_device(): lax.ppermute(physics, 'curve', [(i, (i + k) % SPANS) for i in range(SPANS)])]
    all_to_all x2 -> x1, waiting for transfers between devices: 29.2 us -> 17 us  [per_device(): lax.all_to_all(message.reshape(SPANS, 16, 128), 'curve', split_axis=0, co...]
    gather x16 -> x0, local copies, waits for them, and re-layouts: 10.3 us -> none  [the longest x8 5.79 us: edge_sum(): pieces.append(jnp.take(facing[:, :, side], halo_index[side], axis=-1))]
    all_to_all x2 -> x1, starting transfers between devices: 18.5 us -> 12.1 us  [per_device(): lax.all_to_all(message.reshape(SPANS, 16, 128), 'curve', split_axis=0, co...]
    unnamed x57 -> x20, local copies, waits for them, and re-layouts: 8.96 us -> 3.21 us
    pallas_call x0 -> x5, Pallas kernels: none -> 5.5 us  [the longest x1 1.84 us: per_device(): pl.pallas_call(dynamics_kernel, out_shape=shape((NF, COL, LEV), f32), com...]
    ppermute x4, starting transfers between devices: 2.42 us -> 7.17 us  [per_device(): lax.ppermute(physics, 'curve', [(i, (i + k) % SPANS) for i in range(SPANS)])]
    all_to_all x2 -> x0, other arithmetic: 3.46 us -> none  [the longest x1 1.73 us: per_device(): lax.all_to_all(updated, 'curve', split_axis=2, concat_axis=2, tiled=True)]
  transfers between devices with their start and end apart: 6 -> 5, of which waited for: 6 -> 4; matrix products, arithmetic and copies ran while one was open for 3% -> 0% of each run, Pallas kernels for 0% -> 3%
where the time goes in v1:
time: 51.6 us; the launch traced here: 51.2 us
  waiting for transfers between devices  22.6 us (44%)
  starting transfers between devices  19.2 us (37%)
  Pallas kernels  5.5 us (11%)
  local copies, waits for them, and re-layouts  3.21 us (6%)
  between operations  0.7 us (1%)
    all_to_all x1, waiting for transfers between devices, per_device(): lax.all_to_all(message.reshape(SPANS, 16, 128), 'curve', split_axis=0, co...  17 us
    all_to_all x1, starting transfers between devices, per_device(): lax.all_to_all(message.reshape(SPANS, 16, 128), 'curve', split_axis=0, co...  12.1 us
    ppermute x4, starting transfers between devices, per_device(): lax.ppermute(physics, 'curve', [(i, (i + k) % SPANS) for i in range(SPANS)])  7.17 us
    ppermute x4, waiting for transfers between devices, per_device(): lax.ppermute(physics, 'curve', [(i, (i + k) % SPANS) for i in range(SPANS)])  5.54 us
    unnamed x20, local copies, waits for them, and re-layouts  3.21 us
    pallas_call x1, Pallas kernels, per_device(): pl.pallas_call(dynamics_kernel, out_shape=shape((NF, COL, LEV), f32), com...  1.84 us
    pallas_call x1, Pallas kernels, per_device(): pl.pallas_call(span_kernel, out_shape=(shape((STATE, SLOT), f32), shape((...  1.56 us
    pallas_call x1, Pallas kernels, per_device(): pl.pallas_call(pack_kernel, out_shape=(shape((SLOT * CHUNKS, 128), f32),...  1.26 us
  transfers between devices with their start and end apart: 5, of which 4 were waited for; matrix products, arithmetic and copies ran while one was open for 0% of the time, Pallas kernels for 3%

profile of v1, /device:TPU:16, one launch (start us, length us, event | category | flops | bytes accessed | tf_op | source)
XLA Modules:
  0.0 51.2 jit_solution(17315971844522838091)
XLA Ops:
  0.6 0.0 copy-start.7
  0.6 0.0 copy-start.8
  0.7 0.0 copy-start.9
  0.7 0.7 %copy-done.7 = s32[4,4]{1,0:T(4,128)S(1)} copy-done((s32[4,4]{1,0:T(4,128)S(1)}, s32[4,4]{1,0:T(4,128)}, u32[]{:S(2)}) %copy-start.7) | copy-done | bytes 88
  1.3 0.0 copy-done.8
  1.3 0.0 copy-done.9
  1.3 0.0 copy-start
  1.3 1.0 %copy-done = f32[72,12,64]{0,2,1:T(8,128)S(1)} copy-done((f32[72,12,64]{0,2,1:T(8,128)S(1)}, f32[72,12,64]{0,2,1:T(8,128)}, u32[]{:S(2)}) %copy-start) | copy-done | bytes 221208
  2.3 0.0 copy-start.2
  2.3 0.8 %copy-done.2 = f32[72,128]{1,0:T(8,128)S(1)} copy-done((f32[72,128]{1,0:T(8,128)S(1)}, f32[72,128]{1,0:T(8,128)}, u32[]{:S(2)}) %copy-start.2) | copy-done | bytes 36888
  3.1 0.0 copy-start.4
  3.1 0.8 %copy-done.4 = f32[72,128]{1,0:T(8,128)S(1)} copy-done((f32[72,128]{1,0:T(8,128)S(1)}, f32[72,128]{1,0:T(8,128)}, u32[]{:S(2)}) %copy-start.4) | copy-done | bytes 36888
  3.9 1.3 %pack.1 = (f32[1024,128]{1,0:T(8,128)}, s32[8,128]{1,0:T(8,128)S(1)}) custom-call(f32[12,64,72]{2,1,0:T(8,128)S(1)} %bitcast.11, s32[1,64]{1,0:T(1,128)S(1)} %bitcast.15, f32[72,128]{1,0:T(8,128)S(1)} %copy-done.2, f32[72,128]{1,0:T(8,128)S(1)} %copy-done.4, s32[1,128]{1,0:T(1,128)S(1)} %bitcast.13, s32[4,4]{1,0:T(4,128)S(1)} %copy-done.7), custom_call_target="tpu_custom_call" | custom-call | tf_op jit(solution)/shard_map/pack/pallas_call | solution.py:251
  5.1 0.0 copy-start.1
  5.1 12.1 %all-to-all-start = ((f32[64,16,128]{2,1,0:T(8,128)}), f32[64,16,128]{2,1,0:T(8,128)S(1)}, u32[]{:S(2)}, u32[]{:S(2)}) async-start(f32[64,16,128]{2,1,0:T(8,128)} %bitcast.3), calls=%async_computation | async-start | bytes 1048576 | tf_op jit(solution)/shard_map/all_to_all | solution.py:263
  17.2 0.0 copy-done.1
  17.2 0.1 turn.1.x_ref
  17.4 17.0 %all-to-all-done = f32[64,16,128]{2,1,0:T(8,128)S(1)} async-done(((f32[64,16,128]{2,1,0:T(8,128)}), f32[64,16,128]{2,1,0:T(8,128)S(1)}, u32[]{:S(2)}, u32[]{:S(2)}) %all-to-all-start) | async-done | bytes 524320 | tf_op jit(solution)/shard_map/all_to_all | solution.py:263
  34.4 0.0 copy-start.3
  34.4 0.0 copy-start.5
  34.4 0.0 copy-start.6
  34.4 0.7 %element.1.c_ref = f32[432,128]{1,0:T(8,128)S(1)} custom-call(f32[1024,128]{1,0:T(8,128)S(1)} %bitcast.9, s32[8,128]{1,0:T(8,128)S(1)} %get-tuple-element.8.slot_ref, f32[432,128]{1,0:T(8,128)S(1)} %turn.1.x_ref), custom_call_target="tpu_custom_call" | custom-call | tf_op jit(solution)/shard_map/element/pallas_call | solution.py:266
  35.1 1.6 %collective-permute-start = (f32[432,128]{1,0:T(8,128)S(1)}, f32[432,128]{1,0:T(8,128)S(1)}, u32[]{:S(2)}, u32[]{:S(2)}) collective-permute-start(f32[432,128]{1,0:T(8,128)S(1)} %element.1.c_ref), channel_id=1, source_target_pairs={{0,8},{4,12},{8,16},{12,20},{16,24},{20,28},{24,32},{28,36},{32,40... | collective-permute-start | bytes 663560 | tf_op jit(solution)/shard_map/ppermute | solution.py:280
  36.6 0.0 collective-permute-start.1
  36.6 5.1 %collective-permute-start.2 = (f32[432,128]{1,0:T(8,128)S(1)}, f32[432,128]{1,0:T(8,128)S(1)}, u32[]{:S(2)}, u32[]{:S(2)}) collective-permute-start(f32[432,128]{1,0:T(8,128)S(1)} %element.1.c_ref), channel_id=1, source_target_pairs={{0,252},{4,0},{8,4},{12,8},{16,12},{20,16},{24,20},{28,24},{32,28}... | collective-permute-start | bytes 663560 | tf_op jit(solution)/shard_map/ppermute | solution.py:280
  41.7 0.5 %collective-permute-start.3 = (f32[432,128]{1,0:T(8,128)S(1)}, f32[432,128]{1,0:T(8,128)S(1)}, u32[]{:S(2)}, u32[]{:S(2)}) collective-permute-start(f32[432,128]{1,0:T(8,128)S(1)} %element.1.c_ref), channel_id=1, source_target_pairs={{0,248},{4,252},{8,0},{12,4},{16,8},{20,12},{24,16},{28,20},{32,24... | collective-permute-start | bytes 663560 | tf_op jit(solution)/shard_map/ppermute | solution.py:280
  42.3 0.0 copy-done.3
  42.3 0.0 copy-done.5
  42.3 0.0 copy-done.6
  42.3 1.6 %span.1 = (f32[864,128]{1,0:T(8,128)}, f32[5,128,128]{2,1,0:T(8,128)S(1)}) custom-call(f32[1024,128]{1,0:T(8,128)S(1)} %bitcast.10, f32[72,128]{1,0:T(8,128)S(1)} %copy-done.3, f32[72,128]{1,0:T(8,128)S(1)} %copy-done.5, s32[1,128]{1,0:T(1,128)S(1)} %bitcast.14, f32[64,64]{1,0:T(8,128)S(1)} %copy-done.6), custom_call_target="tpu_custom_call" | custom-call | tf_op jit(solution)/shard_map/span/pallas_call | solution.py:281
  43.8 2.9 %collective-permute-done.a_ref = f32[432,128]{1,0:T(8,128)S(1)} collective-permute-done((f32[432,128]{1,0:T(8,128)S(1)}, f32[432,128]{1,0:T(8,128)S(1)}, u32[]{:S(2)}, u32[]{:S(2)}) %collective-permute-start) | collective-permute-done | bytes 221216 | tf_op jit(solution)/shard_map/ppermute | solution.py:280
  46.7 1.6 %collective-permute-done.1.b_ref = f32[432,128]{1,0:T(8,128)S(1)} collective-permute-done((f32[432,128]{1,0:T(8,128)S(1)}, f32[432,128]{1,0:T(8,128)S(1)}, u32[]{:S(2)}, u32[]{:S(2)}) %collective-permute-start.1) | collective-permute-done | bytes 221216 | tf_op jit(solution)/shard_map/ppermute | solution.py:280
  48.4 0.0 collective-permute-done.2.d_ref
  48.4 1.0 %collective-permute-done.3.e_ref = f32[432,128]{1,0:T(8,128)S(1)} collective-permute-done((f32[432,128]{1,0:T(8,128)S(1)}, f32[432,128]{1,0:T(8,128)S(1)}, u32[]{:S(2)}, u32[]{:S(2)}) %collective-permute-start.3) | collective-permute-done | bytes 221216 | tf_op jit(solution)/shard_map/ppermute | solution.py:280
  49.4 1.8 %dynamics.1 = f32[12,64,72]{2,1,0:T(8,128)} custom-call(f32[432,128]{1,0:T(8,128)S(1)} %collective-permute-done.a_ref, f32[432,128]{1,0:T(8,128)S(1)} %collective-permute-done.1.b_ref, f32[432,128]{1,0:T(8,128)S(1)} %element.1.c_ref, f32[432,128]{1,0:T(8,128)S(1)} %collective-permute-done.2.d_ref, f32[432,128]{1,0:T(8,128)S(1)} %collective-permute-done.3.e_ref, ...), custom_call_target="tpu_custom_call" | custom-call | tf_op jit(solution)/shard_map/dynamics/pallas_call | solution.py:293
Async XLA Ops:
  0.6 0.7 %copy-start.7 = (s32[4,4]{1,0:T(4,128)S(1)}, s32[4,4]{1,0:T(4,128)}, u32[]{:S(2)}) copy-start(s32[4,4]{1,0:T(4,128)} %near_ref.1) | copy-start | bytes 196
  0.6 0.7 %copy-start.8 = (s32[128]{0:T(128)S(1)}, s32[128]{0:T(128)}, u32[]{:S(2)}) copy-start(s32[128]{0:T(128)} %param.11) | copy-start | bytes 1540
  0.7 0.7 %copy-start.9 = (s32[64]{0:T(128)S(1)}, s32[64]{0:T(128)}, u32[]{:S(2)}) copy-start(s32[64]{0:T(128)} %param.8) | copy-start | bytes 772
  1.3 1.0 %copy-start = (f32[72,12,64]{0,2,1:T(8,128)S(1)}, f32[72,12,64]{0,2,1:T(8,128)}, u32[]{:S(2)}) copy-start(f32[72,12,64]{0,2,1:T(8,128)} %param.7) | copy-start | bytes 663556
  2.3 0.8 %copy-start.2 = (f32[72,128]{1,0:T(8,128)S(1)}, f32[72,128]{1,0:T(8,128)}, u32[]{:S(2)}) copy-start(f32[72,128]{1,0:T(8,128)} %diff_ref.3) | copy-start | bytes 110596
  3.1 0.8 %copy-start.4 = (f32[72,128]{1,0:T(8,128)S(1)}, f32[72,128]{1,0:T(8,128)}, u32[]{:S(2)}) copy-start(f32[72,128]{1,0:T(8,128)} %courant_ref.3) | copy-start | bytes 110596
  5.1 12.1 %copy-start.1 = (f32[72,12,64]{0,2,1:T(8,128)S(1)}, f32[72,12,64]{0,2,1:T(8,128)}, u32[]{:S(2)}) copy-start(f32[72,12,64]{0,2,1:T(8,128)} %param.7) | copy-start | bytes 663556
  5.1 29.3 %all-to-all-start = ((f32[64,16,128]{2,1,0:T(8,128)}), f32[64,16,128]{2,1,0:T(8,128)S(1)}, u32[]{:S(2)}, u32[]{:S(2)}) async-start(f32[64,16,128]{2,1,0:T(8,128)} %bitcast.3), calls=%async_computation | async-start | bytes 1048576 | tf_op jit(solution)/shard_map/all_to_all | solution.py:263
  34.4 7.9 %copy-start.3 = (f32[72,128]{1,0:T(8,128)S(1)}, f32[72,128]{1,0:T(8,128)}, u32[]{:S(2)}) copy-start(f32[72,128]{1,0:T(8,128)} %diff_ref.3) | copy-start | bytes 110596
  34.4 7.9 %copy-start.5 = (f32[72,128]{1,0:T(8,128)S(1)}, f32[72,128]{1,0:T(8,128)}, u32[]{:S(2)}) copy-start(f32[72,128]{1,0:T(8,128)} %courant_ref.3) | copy-start | bytes 110596
  34.4 7.9 %copy-start.6 = (f32[64,64]{1,0:T(8,128)S(1)}, f32[64,64]{1,0:T(8,128)}, u32[]{:S(2)}) copy-start(f32[64,64]{1,0:T(8,128)} %constant.2.clone.lap_ref) | copy-start | bytes 49156
  35.1 11.7 %collective-permute-start = (f32[432,128]{1,0:T(8,128)S(1)}, f32[432,128]{1,0:T(8,128)S(1)}, u32[]{:S(2)}, u32[]{:S(2)}) collective-permute-start(f32[432,128]{1,0:T(8,128)S(1)} %element.1.c_ref), channel_id=1, source_target_pairs={{0,8},{4,12},{8,16},{12,20},{16,24},{20,28},{24,32},{28,36},{32,40... | collective-permute-start | bytes 663560 | tf_op jit(solution)/shard_map/ppermute | solution.py:280
  36.6 11.7 %collective-permute-start.1 = (f32[432,128]{1,0:T(8,128)S(1)}, f32[432,128]{1,0:T(8,128)S(1)}, u32[]{:S(2)}, u32[]{:S(2)}) collective-permute-start(f32[432,128]{1,0:T(8,128)S(1)} %element.1.c_ref), channel_id=1, source_target_pairs={{0,4},{4,8},{8,12},{12,16},{16,20},{20,24},{24,28},{28,32},{32,36}... | collective-permute-start | bytes 663560 | tf_op jit(solution)/shard_map/ppermute | solution.py:280
  36.6 11.7 %collective-permute-start.2 = (f32[432,128]{1,0:T(8,128)S(1)}, f32[432,128]{1,0:T(8,128)S(1)}, u32[]{:S(2)}, u32[]{:S(2)}) collective-permute-start(f32[432,128]{1,0:T(8,128)S(1)} %element.1.c_ref), channel_id=1, source_target_pairs={{0,252},{4,0},{8,4},{12,8},{16,12},{20,16},{24,20},{28,24},{32,28}... | collective-permute-start | bytes 663560 | tf_op jit(solution)/shard_map/ppermute | solution.py:280
  41.7 7.7 %collective-permute-start.3 = (f32[432,128]{1,0:T(8,128)S(1)}, f32[432,128]{1,0:T(8,128)S(1)}, u32[]{:S(2)}, u32[]{:S(2)}) collective-permute-start(f32[432,128]{1,0:T(8,128)S(1)} %element.1.c_ref), channel_id=1, source_target_pairs={{0,248},{4,252},{8,0},{12,4},{16,8},{20,12},{24,16},{28,20},{32,24... | collective-permute-start | bytes 663560 | tf_op jit(solution)/shard_map/ppermute | solution.py:280

commit v2 on v1

--- a/solution.py
+++ b/solution.py
@@ -65,24 +65,46 @@
     return jnp.where(level >= LEV - cloud_row, courant, 0.0)
 
 
-def pack_kernel(x_ref, span_ref, diff_ref, courant_ref, cloud_ref, near_ref, out_ref, slot_ref):
+def fetch(sources, targets, sems):
+    copies = [
+        pltpu.make_async_copy(source, target, sems.at[i])
+        for i, (source, target) in enumerate(zip(sources, targets))
+    ]
+    for copy in copies:
+        copy.start()
+    return copies
+
+
+def pack_kernel(
+    x_hbm, span_hbm, diff_hbm, courant_hbm, cloud_hbm, near_hbm, out_ref, slot_ref,
+    x_ref, span_ref, diff_ref, courant_ref, cloud_ref, near_ref, sems,
+):
+    copies = fetch(
+        (span_hbm, cloud_hbm, near_hbm, diff_hbm, courant_hbm, x_hbm),
+        (span_ref, cloud_ref, near_ref, diff_ref, courant_ref, x_ref),
+        sems,
+    )
+    for copy in copies[:5]:
+        copy.wait()
     slot_row = slots_of(span_ref[...])
     slot_ref[...] = jnp.broadcast_to(jnp.concatenate([slot_row, slot_row], axis=1), (8, SLOT))
     pick = (iota((SLOT, COL), 0) == slot_row).astype(f32).astype(bf16)
-    state = jnp.concatenate([x_ref[f] for f in range(NF)], axis=1)
-    hi, mid, lo = split3(state)
-    packed = dot(pick, hi) + dot(pick, mid) + dot(pick, lo)
     diff_t = diff_ref[...].T
     rate_t = active_rate(courant_ref[...], cloud_ref[...]).T
     near = near_ref[...].astype(f32)
     near_row = jnp.concatenate([near[s : s + 1, :] for s in range(4)], axis=1)
     near_t = jnp.broadcast_to(near_row, (SLOT, 16))
+    copies[5].wait()
+    state = jnp.concatenate([x_ref[f] for f in range(NF)], axis=1)
+    hi, mid, lo = split3(state)
+    packed = dot(pick, hi) + dot(pick, mid) + dot(pick, lo)
     message = jnp.concatenate([packed, diff_t, rate_t, near_t], axis=1)
     for k in range(CHUNKS):
         out_ref[pl.ds(k, SLOT, stride=CHUNKS), :] = message[:, 128 * k : 128 * k + 128]
 
 
-def turn_kernel(x_ref, out_ref):
+def turn_kernel(x_hbm, out_ref, x_ref, sems):
+    fetch((x_hbm,), (x_ref,), sems)[0].wait()
     for f in range(PAIR):
         both = jnp.concatenate([x_ref[f], x_ref[f + PAIR]], axis=0)
         out_ref[pl.ds(f * LEV, LEV), :] = both.T
@@ -210,16 +232,24 @@
         inner = dot(lap, second[o * COL : (o + 1) * COL]).astype(bf16)
         matrix = matrix + dot(sums[o].astype(bf16), inner)
     matrix = sums[1] - viscosity * matrix
-    zero = jnp.zeros((COL, COL), f32)
-    for o in range(5):
-        block = matrix[o * COL : (o + 1) * COL]
-        matrix_ref[o] = jnp.concatenate(
-            [jnp.concatenate([block, zero], axis=1), jnp.concatenate([zero, block], axis=1)], axis=0
-        )
+    zero = jnp.zeros((COL, COL), bf16)
+    for place, o in enumerate((2, 1, 3, 0, 4)):
+        halves = []
+        for block in split2(matrix[o * COL : (o + 1) * COL]):
+            top = jnp.concatenate([block, zero], axis=1)
+            bottom = jnp.concatenate([zero, block], axis=1)
+            halves.append(jnp.concatenate([top, bottom], axis=0))
+        matrix_ref[pl.ds(place * 128, 128), :] = jnp.concatenate(halves, axis=1)
+
+
+def apply(x, matrix):
+    hi, lo = split2(x)
+    both = dot(hi, matrix)
+    return both[:, :128] + both[:, 128:] + dot(lo, matrix[:, :128])
 
 
 def span_kernel(
-    recv_ref, diff_ref, courant_ref, cloud_ref, lap_ref, out_ref, matrix_ref,
+    recv_ref, diff_ref, courant_ref, cloud_ref, lap_ref, own_ref, out_ref, matrix_ref, part_sum_ref,
     state_ref, rate_ref, part_ref, ratio_ref,
 ):
     halo_matrix(recv_ref, lap_ref, matrix_ref)
@@ -228,18 +258,32 @@
         state_ref[pl.ds(128 * k, 128), :] = chunk_t(recv_ref, k)
     groups = [strided(state_ref, out_ref, g * PAIR * LEV) for g in range(2)]
     solve(diff_ref, rate_ref, groups, part_ref, ratio_ref)
-
-
-def dynamics_kernel(a_ref, b_ref, c_ref, d_ref, e_ref, matrix_ref, out_ref):
-    total = jnp.zeros((PAIR * LEV, 128), f32)
-    for o, ref in enumerate((a_ref, b_ref, c_ref, d_ref, e_ref)):
-        x_hi, x_lo = split2(ref[...])
-        m_hi, m_lo = split2(matrix_ref[o])
-        total = total + (dot(x_hi, m_hi) + dot(x_lo, m_hi) + dot(x_hi, m_lo))
+    part_sum_ref[...] = apply(own_ref[...], matrix_ref[pl.ds(0, 128), :])
+
+
+def beside_kernel(below_ref, above_ref, part_ref, matrix_ref, out_ref):
+    x = jnp.concatenate([below_ref[...], above_ref[...]], axis=1)
+    out_ref[...] = part_ref[...] + apply(x, matrix_ref[pl.ds(128, 256), :])
+
+
+def beyond_kernel(below_ref, above_ref, part_ref, matrix_ref, out_hbm, out_ref, sems):
+    x = jnp.concatenate([below_ref[...], above_ref[...]], axis=1)
+    total = part_ref[...] + apply(x, matrix_ref[pl.ds(384, 256), :])
+    copies = []
     for f in range(PAIR):
         turned = total[f * LEV : (f + 1) * LEV].T
         out_ref[f] = turned[:COL]
         out_ref[f + PAIR] = turned[COL:]
+        for at in (f, f + PAIR):
+            copy = pltpu.make_async_copy(out_ref.at[at], out_hbm.at[at], sems.at[at])
+            copy.start()
+            copies.append(copy)
+    for copy in copies:
+        copy.wait()
+
+
+def in_hbm(array):
+    return pltpu.with_memory_space_constraint(array, pltpu.HBM)
 
 
 def per_device(column_state, span_of, diffusivity, courant, cloud_levels, neighbors):
@@ -248,18 +292,31 @@
     x = jnp.transpose(column_state, (1, 2, 0))
     span_row = span_of.reshape(1, COL)
     cloud_row = cloud_levels.reshape(1, SLOT)
+    hbm = pl.BlockSpec(memory_space=pltpu.HBM)
     message, slots = pl.pallas_call(
         pack_kernel,
         out_shape=(shape((SLOT * CHUNKS, 128), f32), shape((8, SLOT), jnp.int32)),
+        in_specs=[hbm] * 6,
+        scratch_shapes=[
+            pltpu.VMEM((NF, COL, LEV), f32),
+            pltpu.VMEM((1, COL), jnp.int32),
+            pltpu.VMEM((LEV, SLOT), f32),
+            pltpu.VMEM((LEV, SLOT), f32),
+            pltpu.VMEM((1, SLOT), jnp.int32),
+            pltpu.VMEM((4, 4), jnp.int32),
+            pltpu.SemaphoreType.DMA((6,)),
+        ],
         compiler_params=params,
         name="pack",
-    )(x, span_row, diffusivity, courant, cloud_row, neighbors)
+    )(*(in_hbm(a) for a in (x, span_row, diffusivity, courant, cloud_row, neighbors)))
     turned = pl.pallas_call(
         turn_kernel,
         out_shape=shape((PAIR * LEV, 128), f32),
+        in_specs=[hbm],
+        scratch_shapes=[pltpu.VMEM((NF, COL, LEV), f32), pltpu.SemaphoreType.DMA((1,))],
         compiler_params=params,
         name="turn",
-    )(x)
+    )(in_hbm(x))
     received = lax.all_to_all(
         message.reshape(SPANS, 16, 128), "curve", split_axis=0, concat_axis=0, tiled=True
     ).reshape(SLOT * CHUNKS, 128)
@@ -276,11 +333,13 @@
         name="element",
     )(received, slots, turned)
     halo = {}
-    for k in (2, 1, -1, -2):
+    for k in (1, -1, 2, -2):
         halo[k] = lax.ppermute(physics, "curve", [(i, (i + k) % SPANS) for i in range(SPANS)])
-    span_state, matrix = pl.pallas_call(
+    span_state, matrix, total = pl.pallas_call(
         span_kernel,
-        out_shape=(shape((STATE, SLOT), f32), shape((5, 128, 128), f32)),
+        out_shape=(
+            shape((STATE, SLOT), f32), shape((640, 256), bf16), shape((PAIR * LEV, 128), f32)
+        ),
         scratch_shapes=[
             pltpu.VMEM(((CHUNKS - 1) * 128, 128), f32),
             pltpu.VMEM((LEV, 128), f32),
@@ -289,13 +348,21 @@
         ],
         compiler_params=params,
         name="span",
-    )(received, diffusivity, courant, cloud_row, jnp.asarray(lap_columns))
+    )(received, diffusivity, courant, cloud_row, jnp.asarray(lap_columns), physics)
+    total = pl.pallas_call(
+        beside_kernel,
+        out_shape=shape((PAIR * LEV, 128), f32),
+        compiler_params=params,
+        name="beside",
+    )(halo[1], halo[-1], total, matrix)
     dynamics = pl.pallas_call(
-        dynamics_kernel,
+        beyond_kernel,
         out_shape=shape((NF, COL, LEV), f32),
-        compiler_params=params,
-        name="dynamics",
-    )(halo[2], halo[1], physics, halo[-1], halo[-2], matrix)
+        out_specs=hbm,
+        scratch_shapes=[pltpu.VMEM((NF, COL, LEV), f32), pltpu.SemaphoreType.DMA((NF,))],
+        compiler_params=params,
+        name="beyond",
+    )(halo[2], halo[-2], total, matrix)
     return (
         jnp.transpose(span_state.reshape(NF, LEV, SLOT), (1, 0, 2)),
         jnp.transpose(dynamics, (2, 0, 1)),

time: 51.6 us -> 48.6 us (0.942)
  the two profiles are of different devices: /device:TPU:16 before, /device:TPU:8 now
where the time goes in v2:
time: 48.6 us; the launch traced here: 48.4 us
  starting transfers between devices  22.4 us (46%)
  waiting for transfers between devices  17.5 us (36%)
  Pallas kernels  7.81 us (16%)
  between operations  0.68 us (1%)
    all_to_all x1, waiting for transfers between devices, per_device(): lax.all_to_all(message.reshape(SPANS, 16, 128), 'curve', split_axis=0, co...  16 us
    all_to_all x1, starting transfers between devices, per_device(): lax.all_to_all(message.reshape(SPANS, 16, 128), 'curve', split_axis=0, co...  11.9 us
    ppermute x4, starting transfers between devices, per_device(): lax.ppermute(physics, 'curve', [(i, (i + k) % SPANS) for i in range(SPANS)])  10.5 us
    pallas_call x1, Pallas kernels, per_device(): pl.pallas_call(pack_kernel, out_shape=(shape((SLOT * CHUNKS, 128), f32),...  2.38 us
    pallas_call x1, Pallas kernels, per_device(): pl.pallas_call(span_kernel, out_shape=(shape((STATE, SLOT), f32), shape((...  2.16 us
    ppermute x4, waiting for transfers between devices, per_device(): lax.ppermute(physics, 'curve', [(i, (i + k) % SPANS) for i in range(SPANS)])  1.44 us
    pallas_call x1, Pallas kernels, per_device(): pl.pallas_call(turn_kernel, out_shape=shape((PAIR * LEV, 128), f32), in_s...  1.16 us
    pallas_call x1, Pallas kernels, per_device(): pl.pallas_call(beyond_kernel, out_shape=shape((NF, COL, LEV), f32), out_s...  1.12 us
  transfers between devices with their start and end apart: 5, of which 2 were waited for; matrix products, arithmetic and copies ran while one was open for 0% of the time, Pallas kernels for 7%

profile of v2, /device:TPU:8, one launch (start us, length us, event | category | flops | bytes accessed | tf_op | source)
XLA Modules:
  0.0 48.4 jit_solution(1555675112184492569)
XLA Ops:
  0.6 2.4 %pack.1 = (f32[1024,128]{1,0:T(8,128)}, s32[8,128]{1,0:T(8,128)S(1)}) custom-call(f32[12,64,72]{2,1,0:T(8,128)} %bitcast.13, s32[1,64]{1,0:T(1,128)} %bitcast.16, f32[72,128]{1,0:T(8,128)} %diff_ref.1, f32[72,128]{1,0:T(8,128)} %courant_ref.1, s32[1,128]{1,0:T(1,128)} %bitcast.11, s32[4,4]{1,0:T(4,128)} %near_hbm.1), custom_call_target="tpu_custom_call" | custom-call | tf_op jit(solution)/shard_map/pack/pallas_call | solution.py:296
  3.0 11.9 %all-to-all-start = ((f32[64,16,128]{2,1,0:T(8,128)}), f32[64,16,128]{2,1,0:T(8,128)S(1)}, u32[]{:S(2)}, u32[]{:S(2)}) async-start(f32[64,16,128]{2,1,0:T(8,128)} %bitcast.3), calls=%async_computation | async-start | bytes 1048576 | tf_op jit(solution)/shard_map/all_to_all | solution.py:320
  15.0 1.2 %turn.1.x_ref = f32[432,128]{1,0:T(8,128)S(1)} custom-call(f32[12,64,72]{2,1,0:T(8,128)} %bitcast.14), custom_call_target="tpu_custom_call" | custom-call | tf_op jit(solution)/shard_map/turn/pallas_call | solution.py:312
  16.1 16.0 %all-to-all-done = f32[64,16,128]{2,1,0:T(8,128)S(1)} async-done(((f32[64,16,128]{2,1,0:T(8,128)}), f32[64,16,128]{2,1,0:T(8,128)S(1)}, u32[]{:S(2)}, u32[]{:S(2)}) %all-to-all-start) | async-done | bytes 524320 | tf_op jit(solution)/shard_map/all_to_all | solution.py:320
  32.2 0.0 copy-start
  32.2 0.0 copy-start.1
  32.2 0.0 copy-start.2
  32.2 0.0 copy-start.3
  32.2 0.7 %element.1.own_ref = f32[432,128]{1,0:T(8,128)S(1)} custom-call(f32[1024,128]{1,0:T(8,128)S(1)} %bitcast.9, s32[8,128]{1,0:T(8,128)S(1)} %get-tuple-element.8.slot_ref, f32[432,128]{1,0:T(8,128)S(1)} %turn.1.x_ref), custom_call_target="tpu_custom_call" | custom-call | tf_op jit(solution)/shard_map/element/pallas_call | solution.py:323
  32.9 0.3 collective-permute-start.2
  33.1 4.9 %collective-permute-start.3 = (f32[432,128]{1,0:T(8,128)S(1)}, f32[432,128]{1,0:T(8,128)S(1)}, u32[]{:S(2)}, u32[]{:S(2)}) collective-permute-start(f32[432,128]{1,0:T(8,128)S(1)} %element.1.own_ref), channel_id=1, source_target_pairs={{0,252},{4,0},{8,4},{12,8},{16,12},{20,16},{24,20},{28,24},{32,28}... | collective-permute-start | bytes 663560 | tf_op jit(solution)/shard_map/ppermute | solution.py:337
  38.0 0.0 collective-permute-start
  38.0 5.3 %collective-permute-start.1 = (f32[432,128]{1,0:T(8,128)S(1)}, f32[432,128]{1,0:T(8,128)S(1)}, u32[]{:S(2)}, u32[]{:S(2)}) collective-permute-start(f32[432,128]{1,0:T(8,128)S(1)} %element.1.own_ref), channel_id=1, source_target_pairs={{0,248},{4,252},{8,0},{12,4},{16,8},{20,12},{24,16},{28,20},{32,24... | collective-permute-start | bytes 663560 | tf_op jit(solution)/shard_map/ppermute | solution.py:337
  43.4 0.0 copy-done
  43.4 0.0 copy-done.1
  43.4 0.0 copy-done.2
  43.4 0.0 copy-done.3
  43.4 2.2 %span.1 = (f32[864,128]{1,0:T(8,128)}, bf16[640,256]{1,0:T(8,128)(2,1)S(1)}, f32[432,128]{1,0:T(8,128)S(1)}) custom-call(f32[1024,128]{1,0:T(8,128)S(1)} %bitcast.10, f32[72,128]{1,0:T(8,128)S(1)} %copy-done, f32[72,128]{1,0:T(8,128)S(1)} %copy-done.1, s32[1,128]{1,0:T(1,128)S(1)} %bitcast.12, f32[64,64]{1,0:T(8,128)S(1)} %copy-done.2, ...), custom_call_target="tpu_custom_call" | custom-call | tf_op jit(solution)/shard_map/span/pallas_call | solution.py:338
  45.5 0.0 collective-permute-done.2.below_ref
  45.5 0.0 collective-permute-done.3.above_ref
  45.5 0.3 beside.1.part_ref
  45.8 1.4 %collective-permute-done.below_ref = f32[432,128]{1,0:T(8,128)S(1)} collective-permute-done((f32[432,128]{1,0:T(8,128)S(1)}, f32[432,128]{1,0:T(8,128)S(1)}, u32[]{:S(2)}, u32[]{:S(2)}) %collective-permute-start) | collective-permute-done | bytes 221216 | tf_op jit(solution)/shard_map/ppermute | solution.py:337
  47.3 0.0 collective-permute-done.1.above_ref
  47.3 1.1 %beyond.1 = f32[12,64,72]{2,1,0:T(8,128)} custom-call(f32[432,128]{1,0:T(8,128)S(1)} %collective-permute-done.below_ref, f32[432,128]{1,0:T(8,128)S(1)} %collective-permute-done.1.above_ref, f32[432,128]{1,0:T(8,128)S(1)} %beside.1.part_ref, bf16[640,256]{1,0:T(8,128)(2,1)S(1)} %get-tuple-element.11.matrix_ref), custom_call_target="tpu_custom_call" | custom-call | tf_op jit(solution)/shard_map/beyond/pallas_call | solution.py:358
Async XLA Ops:
  3.0 29.1 %all-to-all-start = ((f32[64,16,128]{2,1,0:T(8,128)}), f32[64,16,128]{2,1,0:T(8,128)S(1)}, u32[]{:S(2)}, u32[]{:S(2)}) async-start(f32[64,16,128]{2,1,0:T(8,128)} %bitcast.3), calls=%async_computation | async-start | bytes 1048576 | tf_op jit(solution)/shard_map/all_to_all | solution.py:320
  32.2 11.2 %copy-start = (f32[72,128]{1,0:T(8,128)S(1)}, f32[72,128]{1,0:T(8,128)}, u32[]{:S(2)}) copy-start(f32[72,128]{1,0:T(8,128)} %diff_ref.1) | copy-start | bytes 110596
  32.2 11.2 %copy-start.1 = (f32[72,128]{1,0:T(8,128)S(1)}, f32[72,128]{1,0:T(8,128)}, u32[]{:S(2)}) copy-start(f32[72,128]{1,0:T(8,128)} %courant_ref.1) | copy-start | bytes 110596
  32.2 11.2 %copy-start.2 = (f32[64,64]{1,0:T(8,128)S(1)}, f32[64,64]{1,0:T(8,128)}, u32[]{:S(2)}) copy-start(f32[64,64]{1,0:T(8,128)} %constant.2.clone.lap_ref) | copy-start | bytes 49156
  32.2 11.2 %copy-start.3 = (s32[128]{0:T(128)S(1)}, s32[128]{0:T(128)}, u32[]{:S(2)}) copy-start(s32[128]{0:T(128)} %param.11) | copy-start | bytes 1540
  32.9 12.7 %collective-permute-start.2 = (f32[432,128]{1,0:T(8,128)S(1)}, f32[432,128]{1,0:T(8,128)S(1)}, u32[]{:S(2)}, u32[]{:S(2)}) collective-permute-start(f32[432,128]{1,0:T(8,128)S(1)} %element.1.own_ref), channel_id=1, source_target_pairs={{0,4},{4,8},{8,12},{12,16},{16,20},{20,24},{24,28},{28,32},{32,36}... | collective-permute-start | bytes 663560 | tf_op jit(solution)/shard_map/ppermute | solution.py:337
  33.1 12.4 %collective-permute-start.3 = (f32[432,128]{1,0:T(8,128)S(1)}, f32[432,128]{1,0:T(8,128)S(1)}, u32[]{:S(2)}, u32[]{:S(2)}) collective-permute-start(f32[432,128]{1,0:T(8,128)S(1)} %element.1.own_ref), channel_id=1, source_target_pairs={{0,252},{4,0},{8,4},{12,8},{16,12},{20,16},{24,20},{28,24},{32,28}... | collective-permute-start | bytes 663560 | tf_op jit(solution)/shard_map/ppermute | solution.py:337
  38.0 9.3 %collective-permute-start = (f32[432,128]{1,0:T(8,128)S(1)}, f32[432,128]{1,0:T(8,128)S(1)}, u32[]{:S(2)}, u32[]{:S(2)}) collective-permute-start(f32[432,128]{1,0:T(8,128)S(1)} %element.1.own_ref), channel_id=1, source_target_pairs={{0,8},{4,12},{8,16},{12,20},{16,24},{20,28},{24,32},{28,36},{32,40... | collective-permute-start | bytes 663560 | tf_op jit(solution)/shard_map/ppermute | solution.py:337
  38.0 9.3 %collective-permute-start.1 = (f32[432,128]{1,0:T(8,128)S(1)}, f32[432,128]{1,0:T(8,128)S(1)}, u32[]{:S(2)}, u32[]{:S(2)}) collective-permute-start(f32[432,128]{1,0:T(8,128)S(1)} %element.1.own_ref), channel_id=1, source_target_pairs={{0,248},{4,252},{8,0},{12,4},{16,8},{20,12},{24,16},{28,20},{32,24... | collective-permute-start | bytes 663560 | tf_op jit(solution)/shard_map/ppermute | solution.py:337

commit v3 on v2

--- a/solution.py
+++ b/solution.py
@@ -185,7 +185,10 @@
     return load, store
 
 
-def element_kernel(recv_ref, slot_ref, x_ref, out_ref, coef_ref, rate_ref, part_ref, ratio_ref):
+def element_kernel(
+    recv_ref, slot_ref, x_ref, out_ref, near_ref, far_ref, coef_ref, rate_ref, part_ref, ratio_ref
+):
+    device = lax.axis_index("curve")
     spread = (iota((SLOT, 128), 0) == slot_ref[0:1, :]).astype(f32).astype(bf16)
     tail = jnp.concatenate([chunk_t(recv_ref, CHUNKS - 2), chunk_t(recv_ref, CHUNKS - 1)], axis=0)
     begin = STATE - 128 * (CHUNKS - 2)
@@ -193,18 +196,43 @@
     columns = dot(hi, spread) + dot(mid, spread) + dot(lo, spread)
     coef_ref[...] = columns[:LEV]
     rate_ref[...] = columns[LEV:]
+    element, relative = neighbour_lanes(recv_ref, device)
+    cuts = []
+    for o, beyond in ((2, 4), (0, 0)):
+        reach = jnp.zeros((COL, COL), f32)
+        for s in range(4):
+            reach = reach + edge_entries(element, relative, o, s, COL, 2)
+        flags = [relative[o][s][:, :32] == beyond for s in range(4)]
+        cuts.append(dot(reach.astype(bf16), corner_choice(flags).astype(bf16)))
+    up, down = cuts
+    odd = lax.rem(device // 2, 2) == 1
+    first, second = jnp.where(odd, down, up), jnp.where(odd, up, down)
+    zero = jnp.zeros((COL, 32), f32)
+    matrix = jnp.concatenate(
+        [
+            jnp.concatenate([first, zero, second, zero], axis=1),
+            jnp.concatenate([zero, first, zero, second], axis=1),
+        ],
+        axis=0,
+    ).astype(bf16)
     solve(coef_ref, rate_ref, [strided(x_ref, out_ref, 0)], part_ref, ratio_ref)
-
-
-def halo_matrix(recv_ref, lap_ref, matrix_ref):
-    device = lax.axis_index("curve")
-    lap = lap_ref[...].astype(bf16)
+    hi, lo = split2(out_ref[...])
+    cut = dot(hi, matrix) + dot(lo, matrix)
+    half = PAIR * LEV // 2
+    near_ref[...] = jnp.concatenate([cut[:half, :COL], cut[half:, :COL]], axis=1)
+    far_ref[...] = jnp.concatenate([cut[:half, COL:], cut[half:, COL:]], axis=1)
+
+
+def edge_places():
     lane = iota((1, COL), 1)
     node = lane // 4
     node_row, node_col = node // 4, node % 4
     on_edge = [node_row == 0, node_col == 3, node_row == 3, node_col == 0]
     facing = [node + 12, node - 3, node - 12, node + 3]
-    edges = sum(jnp.where(edge, 1.0, 0.0) for edge in on_edge)
+    return lane, on_edge, facing
+
+
+def neighbour_lanes(recv_ref, device):
     word = iota((128, 4 * COL), 0) - (128 - 16)
     place = iota((128, 4 * COL), 1)
     spread = (word == (place // COL) * 4 + place % 4).astype(f32).astype(bf16)
@@ -214,32 +242,88 @@
         rows.append(recv_ref[pl.ds(block * 16 + CHUNKS - 1, 1), :])
     rows = jnp.concatenate(rows + [jnp.zeros((5, 128), f32)], axis=0)
     near = dot(rows.astype(bf16), spread).astype(jnp.int32)
+    far = lax.rem(near // 4 - device + (2 + SPANS), SPANS)
+    cut = [slice(s * COL, (s + 1) * COL) for s in range(4)]
+    element = [[near[o : o + 1, c] % 4 for c in cut] for o in range(3)]
+    relative = [[far[o : o + 1, c] for c in cut] for o in range(3)]
+    return element, relative
+
+
+def edge_entries(element, relative, o, s, rows, only=None):
+    lane, on_edge, facing = edge_places()
+    target = facing[s] * 4 + element[o][s]
+    keep = on_edge[s]
+    if only is None:
+        target = target + relative[o][s] * COL
+    else:
+        keep = jnp.logical_and(keep, relative[o][s] == only)
+    target = jnp.where(keep, target, -1)
+    return jnp.where(iota((rows, COL), 0) == target, 0.5, 0.0)
+
+
+def corner_choice(flags):
+    lane = iota((1, 32), 1)
+    j = (lane % 16) // 4
+    up, right = j // 2, j % 2
+    on_row = jnp.where(up == 0, flags[0].astype(f32), flags[2].astype(f32))
+    on_col = jnp.where(right == 0, flags[3].astype(f32), flags[1].astype(f32))
+    place = iota((COL, 32), 0)
+    same = place % 4 == lane % 4
+    node = place // 4
+    corner = jnp.where(node == up * 12 + right * 3, 1.0, 0.0)
+    side = jnp.where(node == (1 + up) * 4 + right * 3, on_row, 0.0)
+    side = side + jnp.where(node == up * 12 + 1 + right, on_col, 0.0)
+    return jnp.where(same, jnp.where(lane < 16, corner, side), 0.0)
+
+
+def twice(block):
+    zero = jnp.zeros(block.shape, block.dtype)
+    top = jnp.concatenate([block, zero], axis=1)
+    return jnp.concatenate([top, jnp.concatenate([zero, block], axis=1)], axis=0)
+
+
+def halo_matrix(recv_ref, lap_ref, matrix_ref, cut_ref):
+    device = lax.axis_index("curve")
+    lap = lap_ref[...].astype(bf16)
+    element, relative = neighbour_lanes(recv_ref, device)
+    lane, on_edge, _ = edge_places()
+    edges = sum(jnp.where(edge, 1.0, 0.0) for edge in on_edge)
     source = iota((5 * COL, COL), 0)
     sums = []
     for o in range(3):
         own = source == lane + (o + 1) * COL
         total = jnp.where(own, 1.0 - 0.5 * edges, 0.0)
         for s in range(4):
-            element = near[o : o + 1, s * COL : (s + 1) * COL]
-            relative = lax.rem(element // 4 - device + (2 + SPANS), SPANS)
-            target = relative * COL + facing[s] * 4 + element % 4
-            target = jnp.where(on_edge[s], target, -1)
-            total = total + jnp.where(source == target, 0.5, 0.0)
+            total = total + edge_entries(element, relative, o, s, 5 * COL)
         sums.append(total)
     second = dot(sums[1][COL : 4 * COL].astype(bf16), lap).astype(bf16)
-    matrix = jnp.zeros((5 * COL, COL), f32)
+    matrix = jnp.zeros((3 * COL, COL), f32)
+    inner = []
     for o in range(3):
-        inner = dot(lap, second[o * COL : (o + 1) * COL]).astype(bf16)
-        matrix = matrix + dot(sums[o].astype(bf16), inner)
-    matrix = sums[1] - viscosity * matrix
-    zero = jnp.zeros((COL, COL), bf16)
-    for place, o in enumerate((2, 1, 3, 0, 4)):
-        halves = []
-        for block in split2(matrix[o * COL : (o + 1) * COL]):
-            top = jnp.concatenate([block, zero], axis=1)
-            bottom = jnp.concatenate([zero, block], axis=1)
-            halves.append(jnp.concatenate([top, bottom], axis=0))
-        matrix_ref[pl.ds(place * 128, 128), :] = jnp.concatenate(halves, axis=1)
+        inner.append(dot(lap, second[o * COL : (o + 1) * COL]).astype(bf16))
+        matrix = matrix + dot(sums[o][COL : 4 * COL].astype(bf16), inner[o])
+    matrix = sums[1][COL : 4 * COL] - viscosity * matrix
+    core = lax.rem(device, 2)
+    for o, place in ((0, 1 + core), (1, 0), (2, 2 - core)):
+        halves = [twice(block) for block in split2(matrix[o * COL : (o + 1) * COL])]
+        start = pl.multiple_of(place * 128, 128)
+        matrix_ref[pl.ds(start, 128), :] = jnp.concatenate(halves, axis=1)
+    parts = []
+    for o in (0, 2):
+        flags = [relative[o][s][:, :32] == 2 for s in range(4)]
+        choice = corner_choice(flags).astype(bf16)
+        parts.append(
+            -viscosity
+            * lax.dot_general(
+                choice, inner[o], (((0,), (0,)), ((), ())), preferred_element_type=f32
+            )
+        )
+    down, up = parts
+    odd = lax.rem(device // 2, 2) == 1
+    far, near = jnp.where(odd, up, down), jnp.where(odd, down, up)
+    for i, block in enumerate((far, near)):
+        for h, half in enumerate(split2(block)):
+            cut_ref[h, pl.ds(i * 128, 128), :] = twice(twice(half))
 
 
 def apply(x, matrix):
@@ -249,10 +333,11 @@
 
 
 def span_kernel(
-    recv_ref, diff_ref, courant_ref, cloud_ref, lap_ref, own_ref, out_ref, matrix_ref, part_sum_ref,
+    recv_ref, diff_ref, courant_ref, cloud_ref, lap_ref, own_ref,
+    out_ref, matrix_ref, cut_ref, part_sum_ref,
     state_ref, rate_ref, part_ref, ratio_ref,
 ):
-    halo_matrix(recv_ref, lap_ref, matrix_ref)
+    halo_matrix(recv_ref, lap_ref, matrix_ref, cut_ref)
     rate_ref[...] = active_rate(courant_ref[...], cloud_ref[...])
     for k in range(CHUNKS - 1):
         state_ref[pl.ds(128 * k, 128), :] = chunk_t(recv_ref, k)
@@ -261,14 +346,15 @@
     part_sum_ref[...] = apply(own_ref[...], matrix_ref[pl.ds(0, 128), :])
 
 
-def beside_kernel(below_ref, above_ref, part_ref, matrix_ref, out_ref):
-    x = jnp.concatenate([below_ref[...], above_ref[...]], axis=1)
+def beside_kernel(across_ref, chip_ref, part_ref, matrix_ref, out_ref):
+    x = jnp.concatenate([across_ref[...], chip_ref[...]], axis=1)
     out_ref[...] = part_ref[...] + apply(x, matrix_ref[pl.ds(128, 256), :])
 
 
-def beyond_kernel(below_ref, above_ref, part_ref, matrix_ref, out_hbm, out_ref, sems):
-    x = jnp.concatenate([below_ref[...], above_ref[...]], axis=1)
-    total = part_ref[...] + apply(x, matrix_ref[pl.ds(384, 256), :])
+def beyond_kernel(far_ref, near_ref, part_ref, cut_ref, out_hbm, out_ref, sems):
+    hi, lo = split2(jnp.concatenate([far_ref[...], near_ref[...]], axis=1))
+    cut = dot(hi, cut_ref[0]) + dot(lo, cut_ref[0]) + dot(hi, cut_ref[1])
+    total = part_ref[...] + jnp.concatenate([cut[:, :128], cut[:, 128:]], axis=0)
     copies = []
     for f in range(PAIR):
         turned = total[f * LEV : (f + 1) * LEV].T
@@ -280,6 +366,10 @@
             copies.append(copy)
     for copy in copies:
         copy.wait()
+
+
+def swap(x, partner):
+    return lax.ppermute(x, "curve", [(i, partner(i) % SPANS) for i in range(SPANS)])
 
 
 def in_hbm(array):
@@ -320,9 +410,11 @@
     received = lax.all_to_all(
         message.reshape(SPANS, 16, 128), "curve", split_axis=0, concat_axis=0, tiled=True
     ).reshape(SLOT * CHUNKS, 128)
-    physics = pl.pallas_call(
+    half = shape((PAIR * LEV // 2, 128), f32)
+    whole = shape((PAIR * LEV, 128), f32)
+    physics, near_cut, far_cut = pl.pallas_call(
         element_kernel,
-        out_shape=shape((PAIR * LEV, 128), f32),
+        out_shape=(whole, half, half),
         scratch_shapes=[
             pltpu.VMEM((LEV, 128), f32),
             pltpu.VMEM((LEV, 128), f32),
@@ -332,13 +424,14 @@
         compiler_params=params,
         name="element",
     )(received, slots, turned)
-    halo = {}
-    for k in (1, -1, 2, -2):
-        halo[k] = lax.ppermute(physics, "curve", [(i, (i + k) % SPANS) for i in range(SPANS)])
-    span_state, matrix, total = pl.pallas_call(
+    across = swap(physics, lambda i: i + 1 if i % 2 else i - 1)
+    chip = swap(physics, lambda i: i ^ 1)
+    far = swap(far_cut, lambda i: i + 2 if i // 2 % 2 else i - 2)
+    near = swap(near_cut, lambda i: i - 2 if i // 2 % 2 else i + 2)
+    span_state, matrix, cut, total = pl.pallas_call(
         span_kernel,
         out_shape=(
-            shape((STATE, SLOT), f32), shape((640, 256), bf16), shape((PAIR * LEV, 128), f32)
+            shape((STATE, SLOT), f32), shape((384, 256), bf16), shape((2, 256, 256), bf16), whole
         ),
         scratch_shapes=[
             pltpu.VMEM(((CHUNKS - 1) * 128, 128), f32),
@@ -351,10 +444,10 @@
     )(received, diffusivity, courant, cloud_row, jnp.asarray(lap_columns), physics)
     total = pl.pallas_call(
         beside_kernel,
-        out_shape=shape((PAIR * LEV, 128), f32),
+        out_shape=whole,
         compiler_params=params,
         name="beside",
-    )(halo[1], halo[-1], total, matrix)
+    )(across, chip, total, matrix)
     dynamics = pl.pallas_call(
         beyond_kernel,
         out_shape=shape((NF, COL, LEV), f32),
@@ -362,7 +455,7 @@
         scratch_shapes=[pltpu.VMEM((NF, COL, LEV), f32), pltpu.SemaphoreType.DMA((NF,))],
         compiler_params=params,
         name="beyond",
-    )(halo[2], halo[-2], total, matrix)
+    )(far, near, total, cut)
     return (
         jnp.transpose(span_state.reshape(NF, LEV, SLOT), (1, 0, 2)),
         jnp.transpose(dynamics, (2, 0, 1)),

time: 48.6 us -> 46.9 us (0.965)
  the two profiles are of different devices: /device:TPU:8 before, /device:TPU:1 now
where the time goes in v3:
time: 46.9 us; the launch traced here: 46.7 us
  waiting for transfers between devices  19.7 us (42%)
  starting transfers between devices  18.1 us (39%)
  Pallas kernels  8.19 us (17%)
  between operations  0.69 us (1%)
    all_to_all x1, waiting for transfers between devices, per_device(): lax.all_to_all(message.reshape(SPANS, 16, 128), 'curve', split_axis=0, co...  16.2 us
    all_to_all x1, starting transfers between devices, per_device(): lax.all_to_all(message.reshape(SPANS, 16, 128), 'curve', split_axis=0, co...  13 us
    ppermute x4, starting transfers between devices, swap(): lax.ppermute(x, 'curve', [(i, partner(i) % SPANS) for i in range(SPANS)])  5.09 us
    ppermute x4, waiting for transfers between devices, swap(): lax.ppermute(x, 'curve', [(i, partner(i) % SPANS) for i in range(SPANS)])  3.56 us
    pallas_call x1, Pallas kernels, per_device(): pl.pallas_call(pack_kernel, out_shape=(shape((SLOT * CHUNKS, 128), f32),...  2.4 us
    pallas_call x1, Pallas kernels, per_device(): pl.pallas_call(span_kernel, out_shape=(shape((STATE, SLOT), f32), shape((...  2.04 us
    pallas_call x1, Pallas kernels, per_device(): pl.pallas_call(beyond_kernel, out_shape=shape((NF, COL, LEV), f32), out_s...  1.19 us
    pallas_call x1, Pallas kernels, per_device(): pl.pallas_call(turn_kernel, out_shape=shape((PAIR * LEV, 128), f32), in_s...  1.16 us
  transfers between devices with their start and end apart: 5, of which 2 were waited for; matrix products, arithmetic and copies ran while one was open for 0% of the time, Pallas kernels for 7%

profile of v3, /device:TPU:1, one launch (start us, length us, event | category | flops | bytes accessed | tf_op | source)
XLA Modules:
  0.0 46.7 jit_solution(14073725416856108649)
XLA Ops:
  0.6 2.4 %pack.1 = (f32[1024,128]{1,0:T(8,128)}, s32[8,128]{1,0:T(8,128)S(1)}) custom-call(f32[12,64,72]{2,1,0:T(8,128)} %bitcast.13, s32[1,64]{1,0:T(1,128)} %bitcast.16, f32[72,128]{1,0:T(8,128)} %diff_ref.1, f32[72,128]{1,0:T(8,128)} %courant_ref.1, s32[1,128]{1,0:T(1,128)} %bitcast.11, s32[4,4]{1,0:T(4,128)} %near_hbm.1), custom_call_target="tpu_custom_call" | custom-call | tf_op jit(solution)/shard_map/pack/pallas_call | solution.py:386
  3.0 13.0 %all-to-all-start = ((f32[64,16,128]{2,1,0:T(8,128)}), f32[64,16,128]{2,1,0:T(8,128)S(1)}, u32[]{:S(2)}, u32[]{:S(2)}) async-start(f32[64,16,128]{2,1,0:T(8,128)} %bitcast.3), calls=%async_computation | async-start | bytes 1048576 | tf_op jit(solution)/shard_map/all_to_all | solution.py:410
  16.0 1.2 %turn.1.x_ref = f32[432,128]{1,0:T(8,128)S(1)} custom-call(f32[12,64,72]{2,1,0:T(8,128)} %bitcast.14), custom_call_target="tpu_custom_call" | custom-call | tf_op jit(solution)/shard_map/turn/pallas_call | solution.py:402
  17.2 16.2 %all-to-all-done = f32[64,16,128]{2,1,0:T(8,128)S(1)} async-done(((f32[64,16,128]{2,1,0:T(8,128)}), f32[64,16,128]{2,1,0:T(8,128)S(1)}, u32[]{:S(2)}, u32[]{:S(2)}) %all-to-all-start) | async-done | bytes 524320 | tf_op jit(solution)/shard_map/all_to_all | solution.py:410
  33.4 0.0 copy-start
  33.4 0.0 copy-start.1
  33.4 0.0 copy-start.2
  33.4 1.1 %element.1 = (f32[432,128]{1,0:T(8,128)S(1)}, f32[216,128]{1,0:T(8,128)S(1)}, f32[216,128]{1,0:T(8,128)S(1)}) custom-call(f32[1024,128]{1,0:T(8,128)S(1)} %bitcast.9, s32[8,128]{1,0:T(8,128)S(1)} %get-tuple-element.12.slot_ref, f32[432,128]{1,0:T(8,128)S(1)} %turn.1.x_ref), custom_call_target="tpu_custom_call" | custom-call | tf_op jit(solution)/shard_map/element/pallas_call | solution.py:415
  34.5 1.5 %collective-permute-start.2 = (f32[432,128]{1,0:T(8,128)S(1)}, f32[432,128]{1,0:T(8,128)S(1)}, u32[]{:S(2)}, u32[]{:S(2)}) collective-permute-start(f32[432,128]{1,0:T(8,128)S(1)} %get-tuple-element.13.own_ref), channel_id=1, source_target_pairs={{0,252},{4,8},{8,4},{12,16},{16,12},{20,24},{24,20},{28,32},{32,28... | collective-permute-start | bytes 663560 | tf_op jit(solution)/shard_map/ppermute | solution.py:372
  36.0 0.7 %collective-permute-start.3 = (f32[432,128]{1,0:T(8,128)S(1)}, f32[432,128]{1,0:T(8,128)S(1)}, u32[]{:S(2)}, u32[]{:S(2)}) collective-permute-start(f32[432,128]{1,0:T(8,128)S(1)} %get-tuple-element.13.own_ref), channel_id=1, source_target_pairs={{0,4},{4,0},{8,12},{12,8},{16,20},{20,16},{24,28},{28,24},{32,36},... | collective-permute-start | bytes 663560 | tf_op jit(solution)/shard_map/ppermute | solution.py:372
  36.7 0.0 copy-start.3
  36.7 2.9 %collective-permute-start = (f32[216,128]{1,0:T(8,128)S(1)}, f32[216,128]{1,0:T(8,128)S(1)}, u32[]{:S(2)}, u32[]{:S(2)}) collective-permute-start(f32[216,128]{1,0:T(8,128)S(1)} %get-tuple-element.15), channel_id=1, source_target_pairs={{0,248},{4,252},{8,16},{12,20},{16,8},{20,12},{24,32},{28,36},{32,... | collective-permute-start | bytes 331784 | tf_op jit(solution)/shard_map/ppermute | solution.py:372
  39.6 0.0 collective-permute-start.1
  39.6 0.0 copy-done
  39.6 0.0 copy-done.1
  39.6 0.0 copy-done.2
  39.6 0.0 copy-done.3
  39.6 2.0 %span.1 = (f32[864,128]{1,0:T(8,128)}, bf16[384,256]{1,0:T(8,128)(2,1)S(1)}, bf16[2,256,256]{2,1,0:T(8,128)(2,1)S(1)}, f32[432,128]{1,0:T(8,128)S(1)}) custom-call(f32[1024,128]{1,0:T(8,128)S(1)} %bitcast.10, f32[72,128]{1,0:T(8,128)S(1)} %copy-done, f32[72,128]{1,0:T(8,128)S(1)} %copy-done.1, s32[1,128]{1,0:T(1,128)S(1)} %bitcast.12, ...), custom_call_target="tpu_custom_call" | custom-call | tf_op jit(solution)/shard_map/span/pallas_call | solution.py:431
  41.6 0.0 collective-permute-done.2.across_ref
  41.7 0.0 collective-permute-done.3.chip_ref
  41.7 0.3 beside.1.part_ref
  42.0 3.5 %collective-permute-done.far_ref = f32[216,128]{1,0:T(8,128)S(1)} collective-permute-done((f32[216,128]{1,0:T(8,128)S(1)}, f32[216,128]{1,0:T(8,128)S(1)}, u32[]{:S(2)}, u32[]{:S(2)}) %collective-permute-start) | collective-permute-done | bytes 110624 | tf_op jit(solution)/shard_map/ppermute | solution.py:372
  45.5 0.0 collective-permute-done.1.near_ref
  45.5 1.2 %beyond.1 = f32[12,64,72]{2,1,0:T(8,128)} custom-call(f32[216,128]{1,0:T(8,128)S(1)} %collective-permute-done.far_ref, f32[216,128]{1,0:T(8,128)S(1)} %collective-permute-done.1.near_ref, f32[432,128]{1,0:T(8,128)S(1)} %beside.1.part_ref, bf16[2,256,256]{2,1,0:T(8,128)(2,1)S(1)} %get-tuple-element.19.cut_ref), custom_call_target="tpu_custom_call" | custom-call | tf_op jit(solution)/shard_map/beyond/pallas_call | solution.py:451
Async XLA Ops:
  3.0 30.3 %all-to-all-start = ((f32[64,16,128]{2,1,0:T(8,128)}), f32[64,16,128]{2,1,0:T(8,128)S(1)}, u32[]{:S(2)}, u32[]{:S(2)}) async-start(f32[64,16,128]{2,1,0:T(8,128)} %bitcast.3), calls=%async_computation | async-start | bytes 1048576 | tf_op jit(solution)/shard_map/all_to_all | solution.py:410
  33.4 6.2 %copy-start = (f32[72,128]{1,0:T(8,128)S(1)}, f32[72,128]{1,0:T(8,128)}, u32[]{:S(2)}) copy-start(f32[72,128]{1,0:T(8,128)} %diff_ref.1) | copy-start | bytes 110596
  33.4 6.2 %copy-start.1 = (f32[72,128]{1,0:T(8,128)S(1)}, f32[72,128]{1,0:T(8,128)}, u32[]{:S(2)}) copy-start(f32[72,128]{1,0:T(8,128)} %courant_ref.1) | copy-start | bytes 110596
  33.4 6.2 %copy-start.2 = (f32[64,64]{1,0:T(8,128)S(1)}, f32[64,64]{1,0:T(8,128)}, u32[]{:S(2)}) copy-start(f32[64,64]{1,0:T(8,128)} %constant.2.clone.lap_ref) | copy-start | bytes 49156
  34.5 7.2 %collective-permute-start.2 = (f32[432,128]{1,0:T(8,128)S(1)}, f32[432,128]{1,0:T(8,128)S(1)}, u32[]{:S(2)}, u32[]{:S(2)}) collective-permute-start(f32[432,128]{1,0:T(8,128)S(1)} %get-tuple-element.13.own_ref), channel_id=1, source_target_pairs={{0,252},{4,8},{8,4},{12,16},{16,12},{20,24},{24,20},{28,32},{32,28... | collective-permute-start | bytes 663560 | tf_op jit(solution)/shard_map/ppermute | solution.py:372
  36.0 5.7 %collective-permute-start.3 = (f32[432,128]{1,0:T(8,128)S(1)}, f32[432,128]{1,0:T(8,128)S(1)}, u32[]{:S(2)}, u32[]{:S(2)}) collective-permute-start(f32[432,128]{1,0:T(8,128)S(1)} %get-tuple-element.13.own_ref), channel_id=1, source_target_pairs={{0,4},{4,0},{8,12},{12,8},{16,20},{20,16},{24,28},{28,24},{32,36},... | collective-permute-start | bytes 663560 | tf_op jit(solution)/shard_map/ppermute | solution.py:372
  36.7 2.9 %copy-start.3 = (s32[128]{0:T(128)S(1)}, s32[128]{0:T(128)}, u32[]{:S(2)}) copy-start(s32[128]{0:T(128)} %param.11) | copy-start | bytes 1540
  36.7 8.8 %collective-permute-start = (f32[216,128]{1,0:T(8,128)S(1)}, f32[216,128]{1,0:T(8,128)S(1)}, u32[]{:S(2)}, u32[]{:S(2)}) collective-permute-start(f32[216,128]{1,0:T(8,128)S(1)} %get-tuple-element.15), channel_id=1, source_target_pairs={{0,248},{4,252},{8,16},{12,20},{16,8},{20,12},{24,32},{28,36},{32,... | collective-permute-start | bytes 331784 | tf_op jit(solution)/shard_map/ppermute | solution.py:372
  39.6 5.9 %collective-permute-start.1 = (f32[216,128]{1,0:T(8,128)S(1)}, f32[216,128]{1,0:T(8,128)S(1)}, u32[]{:S(2)}, u32[]{:S(2)}) collective-permute-start(f32[216,128]{1,0:T(8,128)S(1)} %get-tuple-element.16), channel_id=1, source_target_pairs={{0,8},{4,12},{8,0},{12,4},{16,24},{20,28},{24,16},{28,20},{32,40},... | collective-permute-start | bytes 331784 | tf_op jit(solution)/shard_map/ppermute | solution.py:372

commit v4 on v3

--- a/solution.py
+++ b/solution.py
@@ -76,7 +76,7 @@
 
 
 def pack_kernel(
-    x_hbm, span_hbm, diff_hbm, courant_hbm, cloud_hbm, near_hbm, out_ref, slot_ref,
+    x_hbm, span_hbm, diff_hbm, courant_hbm, cloud_hbm, near_hbm, out_ref, slot_ref, turned_ref,
     x_ref, span_ref, diff_ref, courant_ref, cloud_ref, near_ref, sems,
 ):
     copies = fetch(
@@ -101,13 +101,9 @@
     message = jnp.concatenate([packed, diff_t, rate_t, near_t], axis=1)
     for k in range(CHUNKS):
         out_ref[pl.ds(k, SLOT, stride=CHUNKS), :] = message[:, 128 * k : 128 * k + 128]
-
-
-def turn_kernel(x_hbm, out_ref, x_ref, sems):
-    fetch((x_hbm,), (x_ref,), sems)[0].wait()
     for f in range(PAIR):
         both = jnp.concatenate([x_ref[f], x_ref[f + PAIR]], axis=0)
-        out_ref[pl.ds(f * LEV, LEV), :] = both.T
+        turned_ref[pl.ds(f * LEV, LEV), :] = both.T
 
 
 def chunk_t(recv_ref, k):
@@ -383,9 +379,13 @@
     span_row = span_of.reshape(1, COL)
     cloud_row = cloud_levels.reshape(1, SLOT)
     hbm = pl.BlockSpec(memory_space=pltpu.HBM)
-    message, slots = pl.pallas_call(
+    message, slots, turned = pl.pallas_call(
         pack_kernel,
-        out_shape=(shape((SLOT * CHUNKS, 128), f32), shape((8, SLOT), jnp.int32)),
+        out_shape=(
+            shape((SLOT * CHUNKS, 128), f32),
+            shape((8, SLOT), jnp.int32),
+            shape((PAIR * LEV, 128), f32),
+        ),
         in_specs=[hbm] * 6,
         scratch_shapes=[
             pltpu.VMEM((NF, COL, LEV), f32),
@@ -399,14 +399,6 @@
         compiler_params=params,
         name="pack",
     )(*(in_hbm(a) for a in (x, span_row, diffusivity, courant, cloud_row, neighbors)))
-    turned = pl.pallas_call(
-        turn_kernel,
-        out_shape=shape((PAIR * LEV, 128), f32),
-        in_specs=[hbm],
-        scratch_shapes=[pltpu.VMEM((NF, COL, LEV), f32), pltpu.SemaphoreType.DMA((1,))],
-        compiler_params=params,
-        name="turn",
-    )(in_hbm(x))
     received = lax.all_to_all(
         message.reshape(SPANS, 16, 128), "curve", split_axis=0, concat_axis=0, tiled=True
     ).reshape(SLOT * CHUNKS, 128)

time: 46.9 us -> 45.8 us (0.977)
  blocking collectives: 0 us -> 30.1 us
  waiting for transfers between devices: 19.7 us -> 3.55 us
  starting transfers between devices: 18.1 us -> 5.08 us
  Pallas kernels: 8.19 us -> 6.23 us
    all_to_all x0 -> x1, blocking collectives: none -> 30.1 us  [per_device(): lax.all_to_all(message.reshape(SPANS, 16, 128), 'curve', split_axis=0, co...]
    all_to_all x1 -> x0, waiting for transfers between devices: 16.2 us -> none  [per_device(): lax.all_to_all(message.reshape(SPANS, 16, 128), 'curve', split_axis=0, co...]
    all_to_all x1 -> x0, starting transfers between devices: 13 us -> none  [per_device(): lax.all_to_all(message.reshape(SPANS, 16, 128), 'curve', split_axis=0, co...]
    pallas_call x1 -> x0, Pallas kernels: 1.16 us -> none  [per_device(): pl.pallas_call(turn_kernel, out_shape=shape((PAIR * LEV, 128), f32), in_s...]
    pallas_call x1, Pallas kernels: 2.4 us -> 1.6 us  [per_device(): pl.pallas_call(pack_kernel, out_shape=(shape((SLOT * CHUNKS, 128), f32),...]
  transfers between devices with their start and end apart: 5 -> 4, of which waited for: 2 -> 1; matrix products, arithmetic and copies ran while one was open for 0% -> 0% of each run, Pallas kernels for 7% -> 5%
where the time goes in v4:
time: 45.8 us; the launch traced here: 45.7 us
  blocking collectives  30.1 us (66%)
  Pallas kernels  6.23 us (14%)
  starting transfers between devices  5.08 us (11%)
  waiting for transfers between devices  3.55 us (8%)
  between operations  0.68 us (1%)
    all_to_all x1, blocking collectives, per_device(): lax.all_to_all(message.reshape(SPANS, 16, 128), 'curve', split_axis=0, co...  30.1 us
    ppermute x4, starting transfers between devices, swap(): lax.ppermute(x, 'curve', [(i, partner(i) % SPANS) for i in range(SPANS)])  5.08 us
    ppermute x4, waiting for transfers between devices, swap(): lax.ppermute(x, 'curve', [(i, partner(i) % SPANS) for i in range(SPANS)])  3.55 us
    pallas_call x1, Pallas kernels, per_device(): pl.pallas_call(span_kernel, out_shape=(shape((STATE, SLOT), f32), shape((...  2.04 us
    pallas_call x1, Pallas kernels, per_device(): pl.pallas_call(pack_kernel, out_shape=(shape((SLOT * CHUNKS, 128), f32),...  1.6 us
    pallas_call x1, Pallas kernels, per_device(): pl.pallas_call(beyond_kernel, out_shape=shape((NF, COL, LEV), f32), out_s...  1.19 us
    pallas_call x1, Pallas kernels, per_device(): pl.pallas_call(element_kernel, out_shape=(whole, half, half), scratch_sha...  1.12 us
  transfers between devices with their start and end apart: 4, of which 1 were waited for; matrix products, arithmetic and copies ran while one was open for 0% of the time, Pallas kernels for 5%

profile of v4, /device:TPU:1, one launch (start us, length us, event | category | flops | bytes accessed | tf_op | source)
XLA Modules:
  0.0 45.7 jit_solution(4463606067830762004)
XLA Ops:
  0.6 1.6 %pack.1 = (f32[1024,128]{1,0:T(8,128)S(1)}, s32[8,128]{1,0:T(8,128)S(1)}, f32[432,128]{1,0:T(8,128)S(1)}) custom-call(f32[12,64,72]{2,1,0:T(8,128)} %bitcast.14, s32[1,64]{1,0:T(1,128)} %bitcast.16, f32[72,128]{1,0:T(8,128)} %diff_ref.1, f32[72,128]{1,0:T(8,128)} %courant_ref.1, s32[1,128]{1,0:T(1,128)} %bitcast.12, s32[4,4]{1,0:T(4,128)} %near_hbm.1), custom_call_target="tpu_custom_call" | custom-call | tf_op jit(solution)/shard_map/pack/pallas_call | solution.py:382
  2.2 30.1 %all_to_all.5 = f32[64,16,128]{2,1,0:T(8,128)S(1)} all-to-all(f32[64,16,128]{2,1,0:T(8,128)S(1)} %bitcast.11), channel_id=1, replica_groups=mesh['curve'=64,'field'=4] {'curve'}, dimensions={0} | all-to-all | bytes 1048576 | tf_op jit(solution)/shard_map/all_to_all | solution.py:402
  32.3 0.0 copy-start
  32.3 0.0 copy-start.1
  32.3 0.0 copy-start.2
  32.3 1.1 %element.1 = (f32[432,128]{1,0:T(8,128)S(1)}, f32[216,128]{1,0:T(8,128)S(1)}, f32[216,128]{1,0:T(8,128)S(1)}) custom-call(f32[1024,128]{1,0:T(8,128)S(1)} %bitcast.9, s32[8,128]{1,0:T(8,128)S(1)} %get-tuple-element.13.slot_ref, f32[432,128]{1,0:T(8,128)S(1)} %get-tuple-element.14.x_ref), custom_call_target="tpu_custom_call" | custom-call | tf_op jit(solution)/shard_map/element/pallas_call | solution.py:407
  33.5 1.5 %collective-permute-start.2 = (f32[432,128]{1,0:T(8,128)S(1)}, f32[432,128]{1,0:T(8,128)S(1)}, u32[]{:S(2)}, u32[]{:S(2)}) collective-permute-start(f32[432,128]{1,0:T(8,128)S(1)} %get-tuple-element.15.own_ref), channel_id=1, source_target_pairs={{0,252},{4,8},{8,4},{12,16},{16,12},{20,24},{24,20},{28,32},{32,28... | collective-permute-start | bytes 663560 | tf_op jit(solution)/shard_map/ppermute | solution.py:368
  35.0 0.7 %collective-permute-start.3 = (f32[432,128]{1,0:T(8,128)S(1)}, f32[432,128]{1,0:T(8,128)S(1)}, u32[]{:S(2)}, u32[]{:S(2)}) collective-permute-start(f32[432,128]{1,0:T(8,128)S(1)} %get-tuple-element.15.own_ref), channel_id=1, source_target_pairs={{0,4},{4,0},{8,12},{12,8},{16,20},{20,16},{24,28},{28,24},{32,36},... | collective-permute-start | bytes 663560 | tf_op jit(solution)/shard_map/ppermute | solution.py:368
  35.7 0.0 copy-start.3
  35.7 2.9 %collective-permute-start = (f32[216,128]{1,0:T(8,128)S(1)}, f32[216,128]{1,0:T(8,128)S(1)}, u32[]{:S(2)}, u32[]{:S(2)}) collective-permute-start(f32[216,128]{1,0:T(8,128)S(1)} %get-tuple-element.17), channel_id=1, source_target_pairs={{0,248},{4,252},{8,16},{12,20},{16,8},{20,12},{24,32},{28,36},{32,... | collective-permute-start | bytes 331784 | tf_op jit(solution)/shard_map/ppermute | solution.py:368
  38.6 0.0 collective-permute-start.1
  38.6 0.0 copy-done
  38.6 0.0 copy-done.1
  38.6 0.0 copy-done.2
  38.6 0.0 copy-done.3
  38.6 2.0 %span.1 = (f32[864,128]{1,0:T(8,128)}, bf16[384,256]{1,0:T(8,128)(2,1)S(1)}, bf16[2,256,256]{2,1,0:T(8,128)(2,1)S(1)}, f32[432,128]{1,0:T(8,128)S(1)}) custom-call(f32[1024,128]{1,0:T(8,128)S(1)} %bitcast.10, f32[72,128]{1,0:T(8,128)S(1)} %copy-done, f32[72,128]{1,0:T(8,128)S(1)} %copy-done.1, s32[1,128]{1,0:T(1,128)S(1)} %bitcast.13, ...), custom_call_target="tpu_custom_call" | custom-call | tf_op jit(solution)/shard_map/span/pallas_call | solution.py:423
  40.6 0.0 collective-permute-done.2.across_ref
  40.6 0.0 collective-permute-done.3.chip_ref
  40.6 0.3 beside.1.part_ref
  40.9 3.5 %collective-permute-done.far_ref = f32[216,128]{1,0:T(8,128)S(1)} collective-permute-done((f32[216,128]{1,0:T(8,128)S(1)}, f32[216,128]{1,0:T(8,128)S(1)}, u32[]{:S(2)}, u32[]{:S(2)}) %collective-permute-start) | collective-permute-done | bytes 110624 | tf_op jit(solution)/shard_map/ppermute | solution.py:368
  44.5 0.0 collective-permute-done.1.near_ref
  44.5 1.2 %beyond.1 = f32[12,64,72]{2,1,0:T(8,128)} custom-call(f32[216,128]{1,0:T(8,128)S(1)} %collective-permute-done.far_ref, f32[216,128]{1,0:T(8,128)S(1)} %collective-permute-done.1.near_ref, f32[432,128]{1,0:T(8,128)S(1)} %beside.1.part_ref, bf16[2,256,256]{2,1,0:T(8,128)(2,1)S(1)} %get-tuple-element.21.cut_ref), custom_call_target="tpu_custom_call" | custom-call | tf_op jit(solution)/shard_map/beyond/pallas_call | solution.py:443
Async XLA Ops:
  32.3 6.2 %copy-start = (f32[72,128]{1,0:T(8,128)S(1)}, f32[72,128]{1,0:T(8,128)}, u32[]{:S(2)}) copy-start(f32[72,128]{1,0:T(8,128)} %diff_ref.1) | copy-start | bytes 110596
  32.3 6.2 %copy-start.1 = (f32[72,128]{1,0:T(8,128)S(1)}, f32[72,128]{1,0:T(8,128)}, u32[]{:S(2)}) copy-start(f32[72,128]{1,0:T(8,128)} %courant_ref.1) | copy-start | bytes 110596
  32.3 6.2 %copy-start.2 = (f32[64,64]{1,0:T(8,128)S(1)}, f32[64,64]{1,0:T(8,128)}, u32[]{:S(2)}) copy-start(f32[64,64]{1,0:T(8,128)} %constant.2.clone.lap_ref) | copy-start | bytes 49156
  33.5 7.2 %collective-permute-start.2 = (f32[432,128]{1,0:T(8,128)S(1)}, f32[432,128]{1,0:T(8,128)S(1)}, u32[]{:S(2)}, u32[]{:S(2)}) collective-permute-start(f32[432,128]{1,0:T(8,128)S(1)} %get-tuple-element.15.own_ref), channel_id=1, source_target_pairs={{0,252},{4,8},{8,4},{12,16},{16,12},{20,24},{24,20},{28,32},{32,28... | collective-permute-start | bytes 663560 | tf_op jit(solution)/shard_map/ppermute | solution.py:368
  35.0 5.7 %collective-permute-start.3 = (f32[432,128]{1,0:T(8,128)S(1)}, f32[432,128]{1,0:T(8,128)S(1)}, u32[]{:S(2)}, u32[]{:S(2)}) collective-permute-start(f32[432,128]{1,0:T(8,128)S(1)} %get-tuple-element.15.own_ref), channel_id=1, source_target_pairs={{0,4},{4,0},{8,12},{12,8},{16,20},{20,16},{24,28},{28,24},{32,36},... | collective-permute-start | bytes 663560 | tf_op jit(solution)/shard_map/ppermute | solution.py:368
  35.7 2.9 %copy-start.3 = (s32[128]{0:T(128)S(1)}, s32[128]{0:T(128)}, u32[]{:S(2)}) copy-start(s32[128]{0:T(128)} %param.11) | copy-start | bytes 1540
  35.7 8.8 %collective-permute-start = (f32[216,128]{1,0:T(8,128)S(1)}, f32[216,128]{1,0:T(8,128)S(1)}, u32[]{:S(2)}, u32[]{:S(2)}) collective-permute-start(f32[216,128]{1,0:T(8,128)S(1)} %get-tuple-element.17), channel_id=1, source_target_pairs={{0,248},{4,252},{8,16},{12,20},{16,8},{20,12},{24,32},{28,36},{32,... | collective-permute-start | bytes 331784 | tf_op jit(solution)/shard_map/ppermute | solution.py:368
  38.6 5.9 %collective-permute-start.1 = (f32[216,128]{1,0:T(8,128)S(1)}, f32[216,128]{1,0:T(8,128)S(1)}, u32[]{:S(2)}, u32[]{:S(2)}) collective-permute-start(f32[216,128]{1,0:T(8,128)S(1)} %get-tuple-element.18), channel_id=1, source_target_pairs={{0,8},{4,12},{8,0},{12,4},{16,24},{20,28},{24,16},{28,20},{32,40},... | collective-permute-start | bytes 331784 | tf_op jit(solution)/shard_map/ppermute | solution.py:368

commit v5 on v4

--- a/solution.py
+++ b/solution.py
@@ -96,8 +96,9 @@
     near_t = jnp.broadcast_to(near_row, (SLOT, 16))
     copies[5].wait()
     state = jnp.concatenate([x_ref[f] for f in range(NF)], axis=1)
-    hi, mid, lo = split3(state)
-    packed = dot(pick, hi) + dot(pick, mid) + dot(pick, lo)
+    packed = dot(
+        jnp.concatenate([pick, pick, pick], axis=1), jnp.concatenate(split3(state), axis=0)
+    )
     message = jnp.concatenate([packed, diff_t, rate_t, near_t], axis=1)
     for k in range(CHUNKS):
         out_ref[pl.ds(k, SLOT, stride=CHUNKS), :] = message[:, 128 * k : 128 * k + 128]
@@ -203,20 +204,17 @@
     up, down = cuts
     odd = lax.rem(device // 2, 2) == 1
     first, second = jnp.where(odd, down, up), jnp.where(odd, up, down)
-    zero = jnp.zeros((COL, 32), f32)
-    matrix = jnp.concatenate(
-        [
-            jnp.concatenate([first, zero, second, zero], axis=1),
-            jnp.concatenate([zero, first, zero, second], axis=1),
-        ],
-        axis=0,
-    ).astype(bf16)
+    near, far = twice(first), twice(second)
+    zero = jnp.zeros(near.shape, f32)
+    upper = jnp.concatenate([near, zero, far, zero], axis=1)
+    lower = jnp.concatenate([zero, near, zero, far], axis=1)
+    matrix = jnp.concatenate([upper, lower], axis=0).astype(bf16)
     solve(coef_ref, rate_ref, [strided(x_ref, out_ref, 0)], part_ref, ratio_ref)
-    hi, lo = split2(out_ref[...])
+    half = PAIR * LEV // 2
+    hi, lo = split2(jnp.concatenate([out_ref[:half, :], out_ref[half:, :]], axis=1))
     cut = dot(hi, matrix) + dot(lo, matrix)
-    half = PAIR * LEV // 2
-    near_ref[...] = jnp.concatenate([cut[:half, :COL], cut[half:, :COL]], axis=1)
-    far_ref[...] = jnp.concatenate([cut[:half, COL:], cut[half:, COL:]], axis=1)
+    near_ref[...] = cut[:, :128]
+    far_ref[...] = cut[:, 128:]
 
 
 def edge_places():
@@ -309,17 +307,13 @@
         flags = [relative[o][s][:, :32] == 2 for s in range(4)]
         choice = corner_choice(flags).astype(bf16)
         parts.append(
-            -viscosity
-            * lax.dot_general(
-                choice, inner[o], (((0,), (0,)), ((), ())), preferred_element_type=f32
-            )
+            lax.dot_general(choice, inner[o], (((0,), (0,)), ((), ())), preferred_element_type=f32)
         )
     down, up = parts
     odd = lax.rem(device // 2, 2) == 1
     far, near = jnp.where(odd, up, down), jnp.where(odd, down, up)
     for i, block in enumerate((far, near)):
-        for h, half in enumerate(split2(block)):
-            cut_ref[h, pl.ds(i * 128, 128), :] = twice(twice(half))
+        cut_ref[pl.ds(i * 128, 128), :] = twice(twice(block.astype(bf16)))
 
 
 def apply(x, matrix):
@@ -349,8 +343,8 @@
 
 def beyond_kernel(far_ref, near_ref, part_ref, cut_ref, out_hbm, out_ref, sems):
     hi, lo = split2(jnp.concatenate([far_ref[...], near_ref[...]], axis=1))
-    cut = dot(hi, cut_ref[0]) + dot(lo, cut_ref[0]) + dot(hi, cut_ref[1])
-    total = part_ref[...] + jnp.concatenate([cut[:, :128], cut[:, 128:]], axis=0)
+    cut = dot(hi, cut_ref[...]) + dot(lo, cut_ref[...])
+    total = part_ref[...] - viscosity * jnp.concatenate([cut[:, :128], cut[:, 128:]], axis=0)
     copies = []
     for f in range(PAIR):
         turned = total[f * LEV : (f + 1) * LEV].T
@@ -423,7 +417,7 @@
     span_state, matrix, cut, total = pl.pallas_call(
         span_kernel,
         out_shape=(
-            shape((STATE, SLOT), f32), shape((384, 256), bf16), shape((2, 256, 256), bf16), whole
+            shape((STATE, SLOT), f32), shape((384, 256), bf16), shape((256, 256), bf16), whole
         ),
         scratch_shapes=[
             pltpu.VMEM(((CHUNKS - 1) * 128, 128), f32),

time: 45.8 us -> 45.5 us (level)
  no operation moved by 1% of the time
where the time goes in v5:
time: 45.5 us; the launch traced here: 45.4 us
  blocking collectives  30.1 us (66%)
  Pallas kernels  5.91 us (13%)
  starting transfers between devices  5.09 us (11%)
  waiting for transfers between devices  3.56 us (8%)
  between operations  0.67 us (1%)
    all_to_all x1, blocking collectives, per_device(): lax.all_to_all(message.reshape(SPANS, 16, 128), 'curve', split_axis=0, co...  30.1 us
    ppermute x4, starting transfers between devices, swap(): lax.ppermute(x, 'curve', [(i, partner(i) % SPANS) for i in range(SPANS)])  5.09 us
    ppermute x4, waiting for transfers between devices, swap(): lax.ppermute(x, 'curve', [(i, partner(i) % SPANS) for i in range(SPANS)])  3.56 us
    pallas_call x1, Pallas kernels, per_device(): pl.pallas_call(span_kernel, out_shape=(shape((STATE, SLOT), f32), shape((...  2.03 us
    pallas_call x1, Pallas kernels, per_device(): pl.pallas_call(pack_kernel, out_shape=(shape((SLOT * CHUNKS, 128), f32),...  1.51 us
    pallas_call x1, Pallas kernels, per_device(): pl.pallas_call(beyond_kernel, out_shape=shape((NF, COL, LEV), f32), out_s...  1.12 us
    pallas_call x1, Pallas kernels, per_device(): pl.pallas_call(element_kernel, out_shape=(whole, half, half), scratch_sha...  0.95 us
  transfers between devices with their start and end apart: 4, of which 1 were waited for; matrix products, arithmetic and copies ran while one was open for 0% of the time, Pallas kernels for 5%

profile of v5, /device:TPU:1, one launch (start us, length us, event | category | flops | bytes accessed | tf_op | source)
XLA Modules:
  0.0 45.4 jit_solution(5834129687460295017)
XLA Ops:
  0.6 1.5 %pack.1 = (f32[1024,128]{1,0:T(8,128)S(1)}, s32[8,128]{1,0:T(8,128)S(1)}, f32[432,128]{1,0:T(8,128)S(1)}) custom-call(f32[12,64,72]{2,1,0:T(8,128)} %bitcast.14, s32[1,64]{1,0:T(1,128)} %bitcast.16, f32[72,128]{1,0:T(8,128)} %diff_ref.1, f32[72,128]{1,0:T(8,128)} %courant_ref.1, s32[1,128]{1,0:T(1,128)} %bitcast.12, s32[4,4]{1,0:T(4,128)} %near_hbm.1), custom_call_target="tpu_custom_call" | custom-call | tf_op jit(solution)/shard_map/pack/pallas_call | solution.py:376
  2.1 30.1 %all_to_all.5 = f32[64,16,128]{2,1,0:T(8,128)S(1)} all-to-all(f32[64,16,128]{2,1,0:T(8,128)S(1)} %bitcast.11), channel_id=1, replica_groups=mesh['curve'=64,'field'=4] {'curve'}, dimensions={0} | all-to-all | bytes 1048576 | tf_op jit(solution)/shard_map/all_to_all | solution.py:396
  32.3 0.0 copy-start
  32.3 0.0 copy-start.1
  32.3 0.0 copy-start.2
  32.3 1.0 %element.1 = (f32[432,128]{1,0:T(8,128)S(1)}, f32[216,128]{1,0:T(8,128)S(1)}, f32[216,128]{1,0:T(8,128)S(1)}) custom-call(f32[1024,128]{1,0:T(8,128)S(1)} %bitcast.9, s32[8,128]{1,0:T(8,128)S(1)} %get-tuple-element.13.slot_ref, f32[432,128]{1,0:T(8,128)S(1)} %get-tuple-element.14.x_ref), custom_call_target="tpu_custom_call" | custom-call | tf_op jit(solution)/shard_map/element/pallas_call | solution.py:401
  33.2 1.5 %collective-permute-start.2 = (f32[432,128]{1,0:T(8,128)S(1)}, f32[432,128]{1,0:T(8,128)S(1)}, u32[]{:S(2)}, u32[]{:S(2)}) collective-permute-start(f32[432,128]{1,0:T(8,128)S(1)} %get-tuple-element.15.own_ref), channel_id=1, source_target_pairs={{0,252},{4,8},{8,4},{12,16},{16,12},{20,24},{24,20},{28,32},{32,28... | collective-permute-start | bytes 663560 | tf_op jit(solution)/shard_map/ppermute | solution.py:362
  34.7 0.7 %collective-permute-start.3 = (f32[432,128]{1,0:T(8,128)S(1)}, f32[432,128]{1,0:T(8,128)S(1)}, u32[]{:S(2)}, u32[]{:S(2)}) collective-permute-start(f32[432,128]{1,0:T(8,128)S(1)} %get-tuple-element.15.own_ref), channel_id=1, source_target_pairs={{0,4},{4,0},{8,12},{12,8},{16,20},{20,16},{24,28},{28,24},{32,36},... | collective-permute-start | bytes 663560 | tf_op jit(solution)/shard_map/ppermute | solution.py:362
  35.4 0.0 copy-start.3
  35.4 2.9 %collective-permute-start = (f32[216,128]{1,0:T(8,128)S(1)}, f32[216,128]{1,0:T(8,128)S(1)}, u32[]{:S(2)}, u32[]{:S(2)}) collective-permute-start(f32[216,128]{1,0:T(8,128)S(1)} %get-tuple-element.17), channel_id=1, source_target_pairs={{0,248},{4,252},{8,16},{12,20},{16,8},{20,12},{24,32},{28,36},{32,... | collective-permute-start | bytes 331784 | tf_op jit(solution)/shard_map/ppermute | solution.py:362
  38.3 0.0 collective-permute-start.1
  38.3 0.0 copy-done
  38.3 0.0 copy-done.1
  38.3 0.0 copy-done.2
  38.3 0.0 copy-done.3
  38.3 2.0 %span.1 = (f32[864,128]{1,0:T(8,128)}, bf16[384,256]{1,0:T(8,128)(2,1)S(1)}, bf16[256,256]{1,0:T(8,128)(2,1)S(1)}, f32[432,128]{1,0:T(8,128)S(1)}) custom-call(f32[1024,128]{1,0:T(8,128)S(1)} %bitcast.10, f32[72,128]{1,0:T(8,128)S(1)} %copy-done, f32[72,128]{1,0:T(8,128)S(1)} %copy-done.1, s32[1,128]{1,0:T(1,128)S(1)} %bitcast.13, f32[64,64]{1,0:T(8,128)S(1)} %copy-done.2, ...), custom_call_target="tpu_custom_call" | custom-call | tf_op jit(solution)/shard_map/span/pallas_call | solution.py:417
  40.4 0.0 collective-permute-done.2.across_ref
  40.4 0.0 collective-permute-done.3.chip_ref
  40.4 0.3 beside.1.part_ref
  40.7 3.6 %collective-permute-done.far_ref = f32[216,128]{1,0:T(8,128)S(1)} collective-permute-done((f32[216,128]{1,0:T(8,128)S(1)}, f32[216,128]{1,0:T(8,128)S(1)}, u32[]{:S(2)}, u32[]{:S(2)}) %collective-permute-start) | collective-permute-done | bytes 110624 | tf_op jit(solution)/shard_map/ppermute | solution.py:362
  44.2 0.0 collective-permute-done.1.near_ref
  44.2 1.1 %beyond.1 = f32[12,64,72]{2,1,0:T(8,128)} custom-call(f32[216,128]{1,0:T(8,128)S(1)} %collective-permute-done.far_ref, f32[216,128]{1,0:T(8,128)S(1)} %collective-permute-done.1.near_ref, f32[432,128]{1,0:T(8,128)S(1)} %beside.1.part_ref, bf16[256,256]{1,0:T(8,128)(2,1)S(1)} %get-tuple-element.21.cut_ref), custom_call_target="tpu_custom_call" | custom-call | tf_op jit(solution)/shard_map/beyond/pallas_call | solution.py:437
Async XLA Ops:
  32.3 6.1 %copy-start = (f32[72,128]{1,0:T(8,128)S(1)}, f32[72,128]{1,0:T(8,128)}, u32[]{:S(2)}) copy-start(f32[72,128]{1,0:T(8,128)} %diff_ref.1) | copy-start | bytes 110596
  32.3 6.1 %copy-start.1 = (f32[72,128]{1,0:T(8,128)S(1)}, f32[72,128]{1,0:T(8,128)}, u32[]{:S(2)}) copy-start(f32[72,128]{1,0:T(8,128)} %courant_ref.1) | copy-start | bytes 110596
  32.3 6.1 %copy-start.2 = (f32[64,64]{1,0:T(8,128)S(1)}, f32[64,64]{1,0:T(8,128)}, u32[]{:S(2)}) copy-start(f32[64,64]{1,0:T(8,128)} %constant.2.clone.lap_ref) | copy-start | bytes 49156
  33.2 7.2 %collective-permute-start.2 = (f32[432,128]{1,0:T(8,128)S(1)}, f32[432,128]{1,0:T(8,128)S(1)}, u32[]{:S(2)}, u32[]{:S(2)}) collective-permute-start(f32[432,128]{1,0:T(8,128)S(1)} %get-tuple-element.15.own_ref), channel_id=1, source_target_pairs={{0,252},{4,8},{8,4},{12,16},{16,12},{20,24},{24,20},{28,32},{32,28... | collective-permute-start | bytes 663560 | tf_op jit(solution)/shard_map/ppermute | solution.py:362
  34.7 5.7 %collective-permute-start.3 = (f32[432,128]{1,0:T(8,128)S(1)}, f32[432,128]{1,0:T(8,128)S(1)}, u32[]{:S(2)}, u32[]{:S(2)}) collective-permute-start(f32[432,128]{1,0:T(8,128)S(1)} %get-tuple-element.15.own_ref), channel_id=1, source_target_pairs={{0,4},{4,0},{8,12},{12,8},{16,20},{20,16},{24,28},{28,24},{32,36},... | collective-permute-start | bytes 663560 | tf_op jit(solution)/shard_map/ppermute | solution.py:362
  35.4 2.9 %copy-start.3 = (s32[128]{0:T(128)S(1)}, s32[128]{0:T(128)}, u32[]{:S(2)}) copy-start(s32[128]{0:T(128)} %param.11) | copy-start | bytes 1540
  35.4 8.8 %collective-permute-start = (f32[216,128]{1,0:T(8,128)S(1)}, f32[216,128]{1,0:T(8,128)S(1)}, u32[]{:S(2)}, u32[]{:S(2)}) collective-permute-start(f32[216,128]{1,0:T(8,128)S(1)} %get-tuple-element.17), channel_id=1, source_target_pairs={{0,248},{4,252},{8,16},{12,20},{16,8},{20,12},{24,32},{28,36},{32,... | collective-permute-start | bytes 331784 | tf_op jit(solution)/shard_map/ppermute | solution.py:362
  38.3 5.9 %collective-permute-start.1 = (f32[216,128]{1,0:T(8,128)S(1)}, f32[216,128]{1,0:T(8,128)S(1)}, u32[]{:S(2)}, u32[]{:S(2)}) collective-permute-start(f32[216,128]{1,0:T(8,128)S(1)} %get-tuple-element.18), channel_id=1, source_target_pairs={{0,8},{4,12},{8,0},{12,4},{16,24},{20,28},{24,16},{28,20},{32,40},... | collective-permute-start | bytes 331784 | tf_op jit(solution)/shard_map/ppermute | solution.py:362

commit v6 on v5

--- a/solution.py
+++ b/solution.py
@@ -183,7 +183,7 @@
 
 
 def element_kernel(
-    recv_ref, slot_ref, x_ref, out_ref, near_ref, far_ref, coef_ref, rate_ref, part_ref, ratio_ref
+    recv_ref, slot_ref, x_ref, out_ref, cut_ref, coef_ref, rate_ref, part_ref, ratio_ref
 ):
     device = lax.axis_index("curve")
     spread = (iota((SLOT, 128), 0) == slot_ref[0:1, :]).astype(f32).astype(bf16)
@@ -208,11 +208,14 @@
     zero = jnp.zeros(near.shape, f32)
     upper = jnp.concatenate([near, zero, far, zero], axis=1)
     lower = jnp.concatenate([zero, near, zero, far], axis=1)
-    matrix = jnp.concatenate([upper, lower], axis=0).astype(bf16)
+    cut_ref[...] = jnp.concatenate([upper, lower], axis=0).astype(bf16)
     solve(coef_ref, rate_ref, [strided(x_ref, out_ref, 0)], part_ref, ratio_ref)
+
+
+def cut_kernel(x_ref, matrix_ref, near_ref, far_ref):
     half = PAIR * LEV // 2
-    hi, lo = split2(jnp.concatenate([out_ref[:half, :], out_ref[half:, :]], axis=1))
-    cut = dot(hi, matrix) + dot(lo, matrix)
+    hi, lo = split2(jnp.concatenate([x_ref[:half, :], x_ref[half:, :]], axis=1))
+    cut = dot(hi, matrix_ref[...]) + dot(lo, matrix_ref[...])
     near_ref[...] = cut[:, :128]
     far_ref[...] = cut[:, 128:]
 
@@ -398,9 +401,9 @@
     ).reshape(SLOT * CHUNKS, 128)
     half = shape((PAIR * LEV // 2, 128), f32)
     whole = shape((PAIR * LEV, 128), f32)
-    physics, near_cut, far_cut = pl.pallas_call(
+    physics, cut_matrix = pl.pallas_call(
         element_kernel,
-        out_shape=(whole, half, half),
+        out_shape=(whole, shape((256, 256), bf16)),
         scratch_shapes=[
             pltpu.VMEM((LEV, 128), f32),
             pltpu.VMEM((LEV, 128), f32),
@@ -410,8 +413,15 @@
         compiler_params=params,
         name="element",
     )(received, slots, turned)
+    near_cut, far_cut = pl.pallas_call(
+        cut_kernel,
+        out_shape=(half, half),
+        compiler_params=params,
+        name="cut",
+    )(physics, cut_matrix)
     across = swap(physics, lambda i: i + 1 if i % 2 else i - 1)
-    chip = swap(physics, lambda i: i ^ 1)
+    again, near_cut = lax.optimization_barrier((physics, near_cut))
+    chip = swap(again, lambda i: i ^ 1)
     far = swap(far_cut, lambda i: i + 2 if i // 2 % 2 else i - 2)
     near = swap(near_cut, lambda i: i - 2 if i // 2 % 2 else i + 2)
     span_state, matrix, cut, total = pl.pallas_call(

time: 45.5 us -> 44.8 us (0.985)
  waiting for transfers between devices: 3.56 us -> 2.72 us
    ppermute x4, waiting for transfers between devices: 3.56 us -> 2.72 us  [swap(): lax.ppermute(x, 'curve', [(i, partner(i) % SPANS) for i in range(SPANS)])]
    pallas_call x1 -> x2, Pallas kernels: 0.95 us -> 0.96 us  [the longest x1 0.74 us: per_device(): pl.pallas_call(element_kernel, out_shape=(whole, shape((256, 256), bf16))...]
  transfers between devices with their start and end apart: 4 -> 4, of which waited for: 1 -> 1; matrix products, arithmetic and copies ran while one was open for 0% -> 0% of each run, Pallas kernels for 5% -> 6%
where the time goes in v6:
time: 44.8 us; the launch traced here: 44.7 us
  blocking collectives  30.1 us (67%)
  Pallas kernels  5.91 us (13%)
  starting transfers between devices  5.27 us (12%)
  waiting for transfers between devices  2.72 us (6%)
  between operations  0.69 us (2%)
    all_to_all x1, blocking collectives, per_device(): lax.all_to_all(message.reshape(SPANS, 16, 128), 'curve', split_axis=0, co...  30.1 us
    ppermute x4, starting transfers between devices, swap(): lax.ppermute(x, 'curve', [(i, partner(i) % SPANS) for i in range(SPANS)])  5.27 us
    ppermute x4, waiting for transfers between devices, swap(): lax.ppermute(x, 'curve', [(i, partner(i) % SPANS) for i in range(SPANS)])  2.72 us
    pallas_call x1, Pallas kernels, per_device(): pl.pallas_call(span_kernel, out_shape=(shape((STATE, SLOT), f32), shape((...  2.03 us
    pallas_call x1, Pallas kernels, per_device(): pl.pallas_call(pack_kernel, out_shape=(shape((SLOT * CHUNKS, 128), f32),...  1.51 us
    pallas_call x1, Pallas kernels, per_device(): pl.pallas_call(beyond_kernel, out_shape=shape((NF, COL, LEV), f32), out_s...  1.12 us
  transfers between devices with their start and end apart: 4, of which 1 were waited for; matrix products, arithmetic and copies ran while one was open for 0% of the time, Pallas kernels for 6%

profile of v6, /device:TPU:1, one launch (start us, length us, event | category | flops | bytes accessed | tf_op | source)
XLA Modules:
  0.0 44.7 jit_solution(5999238889314123828)
XLA Ops:
  0.6 1.5 %pack.1 = (f32[1024,128]{1,0:T(8,128)S(1)}, s32[8,128]{1,0:T(8,128)S(1)}, f32[432,128]{1,0:T(8,128)S(1)}) custom-call(f32[12,64,72]{2,1,0:T(8,128)} %bitcast.14, s32[1,64]{1,0:T(1,128)} %bitcast.16, f32[72,128]{1,0:T(8,128)} %diff_ref.1, f32[72,128]{1,0:T(8,128)} %courant_ref.1, s32[1,128]{1,0:T(1,128)} %bitcast.12, s32[4,4]{1,0:T(4,128)} %near_hbm.1), custom_call_target="tpu_custom_call" | custom-call | tf_op jit(solution)/shard_map/pack/pallas_call | solution.py:379
  2.1 30.1 %all_to_all.5 = f32[64,16,128]{2,1,0:T(8,128)S(1)} all-to-all(f32[64,16,128]{2,1,0:T(8,128)S(1)} %bitcast.11), channel_id=1, replica_groups=mesh['curve'=64,'field'=4] {'curve'}, dimensions={0} | all-to-all | bytes 1048576 | tf_op jit(solution)/shard_map/all_to_all | solution.py:399
  32.3 0.7 %element.1 = (f32[432,128]{1,0:T(8,128)S(1)}, bf16[256,256]{1,0:T(8,128)(2,1)S(1)}) custom-call(f32[1024,128]{1,0:T(8,128)S(1)} %bitcast.9, s32[8,128]{1,0:T(8,128)S(1)} %get-tuple-element.16.slot_ref, f32[432,128]{1,0:T(8,128)S(1)} %get-tuple-element.17.x_ref), custom_call_target="tpu_custom_call" | custom-call | tf_op jit(solution)/shard_map/element/pallas_call | solution.py:404
  33.0 1.5 %collective-permute-start.2 = (f32[432,128]{1,0:T(8,128)S(1)}, f32[432,128]{1,0:T(8,128)S(1)}, u32[]{:S(2)}, u32[]{:S(2)}) collective-permute-start(f32[432,128]{1,0:T(8,128)S(1)} %get-tuple-element.24.own_ref.x_ref), channel_id=1, source_target_pairs={{0,252},{4,8},{8,4},{12,16},{16,12},{20,24},{24,20},{28,32},{32,28... | collective-permute-start | bytes 663560 | tf_op jit(solution)/shard_map/ppermute | solution.py:365
  34.5 0.0 copy-start
  34.5 0.0 copy-start.1
  34.5 0.0 copy-start.2
  34.5 0.2 cut.1
  34.7 0.0 copy-start.3
  34.7 0.8 %collective-permute-start.3 = (f32[432,128]{1,0:T(8,128)S(1)}, f32[432,128]{1,0:T(8,128)S(1)}, u32[]{:S(2)}, u32[]{:S(2)}) collective-permute-start(f32[432,128]{1,0:T(8,128)S(1)} %get-tuple-element.24.own_ref.x_ref), channel_id=1, source_target_pairs={{0,4},{4,0},{8,12},{12,8},{16,20},{20,16},{24,28},{28,24},{32,36},... | collective-permute-start | bytes 663560 | tf_op jit(solution)/shard_map/ppermute | solution.py:365
  35.5 3.0 %collective-permute-start = (f32[216,128]{1,0:T(8,128)S(1)}, f32[216,128]{1,0:T(8,128)S(1)}, u32[]{:S(2)}, u32[]{:S(2)}) collective-permute-start(f32[216,128]{1,0:T(8,128)S(1)} %get-tuple-element.21), channel_id=1, source_target_pairs={{0,248},{4,252},{8,16},{12,20},{16,8},{20,12},{24,32},{28,36},{32,... | collective-permute-start | bytes 331784 | tf_op jit(solution)/shard_map/ppermute | solution.py:365
  38.5 0.0 collective-permute-start.1
  38.5 0.0 copy-done
  38.5 0.0 copy-done.1
  38.5 0.0 copy-done.2
  38.5 0.0 copy-done.3
  38.5 2.0 %span.1 = (f32[864,128]{1,0:T(8,128)}, bf16[384,256]{1,0:T(8,128)(2,1)S(1)}, bf16[256,256]{1,0:T(8,128)(2,1)S(1)}, f32[432,128]{1,0:T(8,128)S(1)}) custom-call(f32[1024,128]{1,0:T(8,128)S(1)} %bitcast.10, f32[72,128]{1,0:T(8,128)S(1)} %copy-done, f32[72,128]{1,0:T(8,128)S(1)} %copy-done.1, s32[1,128]{1,0:T(1,128)S(1)} %bitcast.13, f32[64,64]{1,0:T(8,128)S(1)} %copy-done.2, ...), custom_call_target="tpu_custom_call" | custom-call | tf_op jit(solution)/shard_map/span/pallas_call | solution.py:427
  40.6 0.0 collective-permute-done.2.across_ref
  40.6 0.0 collective-permute-done.3.chip_ref
  40.6 0.3 beside.1.part_ref
  40.9 2.7 %collective-permute-done.far_ref = f32[216,128]{1,0:T(8,128)S(1)} collective-permute-done((f32[216,128]{1,0:T(8,128)S(1)}, f32[216,128]{1,0:T(8,128)S(1)}, u32[]{:S(2)}, u32[]{:S(2)}) %collective-permute-start) | collective-permute-done | bytes 110624 | tf_op jit(solution)/shard_map/ppermute | solution.py:365
  43.6 0.0 collective-permute-done.1.near_ref
  43.6 1.1 %beyond.1 = f32[12,64,72]{2,1,0:T(8,128)} custom-call(f32[216,128]{1,0:T(8,128)S(1)} %collective-permute-done.far_ref, f32[216,128]{1,0:T(8,128)S(1)} %collective-permute-done.1.near_ref, f32[432,128]{1,0:T(8,128)S(1)} %beside.1.part_ref, bf16[256,256]{1,0:T(8,128)(2,1)S(1)} %get-tuple-element.27.cut_ref), custom_call_target="tpu_custom_call" | custom-call | tf_op jit(solution)/shard_map/beyond/pallas_call | solution.py:447
Async XLA Ops:
  33.0 7.6 %collective-permute-start.2 = (f32[432,128]{1,0:T(8,128)S(1)}, f32[432,128]{1,0:T(8,128)S(1)}, u32[]{:S(2)}, u32[]{:S(2)}) collective-permute-start(f32[432,128]{1,0:T(8,128)S(1)} %get-tuple-element.24.own_ref.x_ref), channel_id=1, source_target_pairs={{0,252},{4,8},{8,4},{12,16},{16,12},{20,24},{24,20},{28,32},{32,28... | collective-permute-start | bytes 663560 | tf_op jit(solution)/shard_map/ppermute | solution.py:365
  34.5 4.0 %copy-start = (f32[72,128]{1,0:T(8,128)S(1)}, f32[72,128]{1,0:T(8,128)}, u32[]{:S(2)}) copy-start(f32[72,128]{1,0:T(8,128)} %diff_ref.1) | copy-start | bytes 110596
  34.5 4.0 %copy-start.1 = (f32[72,128]{1,0:T(8,128)S(1)}, f32[72,128]{1,0:T(8,128)}, u32[]{:S(2)}) copy-start(f32[72,128]{1,0:T(8,128)} %courant_ref.1) | copy-start | bytes 110596
  34.5 4.0 %copy-start.2 = (f32[64,64]{1,0:T(8,128)S(1)}, f32[64,64]{1,0:T(8,128)}, u32[]{:S(2)}) copy-start(f32[64,64]{1,0:T(8,128)} %constant.2.clone.lap_ref) | copy-start | bytes 49156
  34.7 3.8 %copy-start.3 = (s32[128]{0:T(128)S(1)}, s32[128]{0:T(128)}, u32[]{:S(2)}) copy-start(s32[128]{0:T(128)} %param.11) | copy-start | bytes 1540
  34.7 5.8 %collective-permute-start.3 = (f32[432,128]{1,0:T(8,128)S(1)}, f32[432,128]{1,0:T(8,128)S(1)}, u32[]{:S(2)}, u32[]{:S(2)}) collective-permute-start(f32[432,128]{1,0:T(8,128)S(1)} %get-tuple-element.24.own_ref.x_ref), channel_id=1, source_target_pairs={{0,4},{4,0},{8,12},{12,8},{16,20},{20,16},{24,28},{28,24},{32,36},... | collective-permute-start | bytes 663560 | tf_op jit(solution)/shard_map/ppermute | solution.py:365
  35.5 8.1 %collective-permute-start = (f32[216,128]{1,0:T(8,128)S(1)}, f32[216,128]{1,0:T(8,128)S(1)}, u32[]{:S(2)}, u32[]{:S(2)}) collective-permute-start(f32[216,128]{1,0:T(8,128)S(1)} %get-tuple-element.21), channel_id=1, source_target_pairs={{0,248},{4,252},{8,16},{12,20},{16,8},{20,12},{24,32},{28,36},{32,... | collective-permute-start | bytes 331784 | tf_op jit(solution)/shard_map/ppermute | solution.py:365
  38.5 5.1 %collective-permute-start.1 = (f32[216,128]{1,0:T(8,128)S(1)}, f32[216,128]{1,0:T(8,128)S(1)}, u32[]{:S(2)}, u32[]{:S(2)}) collective-permute-start(f32[216,128]{1,0:T(8,128)S(1)} %get-tuple-element.23), channel_id=1, source_target_pairs={{0,8},{4,12},{8,0},{12,4},{16,24},{20,28},{24,16},{28,20},{32,40},... | collective-permute-start | bytes 331784 | tf_op jit(solution)/shard_map/ppermute | solution.py:365

commit v7 on v6

--- a/solution.py
+++ b/solution.py
@@ -187,12 +187,16 @@
 ):
     device = lax.axis_index("curve")
     spread = (iota((SLOT, 128), 0) == slot_ref[0:1, :]).astype(f32).astype(bf16)
-    tail = jnp.concatenate([chunk_t(recv_ref, CHUNKS - 2), chunk_t(recv_ref, CHUNKS - 1)], axis=0)
+    tail = jnp.concatenate(
+        [recv_ref[pl.ds(k, SLOT, stride=CHUNKS), :] for k in (CHUNKS - 2, CHUNKS - 1)], axis=1
+    )
     begin = STATE - 128 * (CHUNKS - 2)
-    hi, mid, lo = split3(tail[begin : begin + 2 * LEV])
-    columns = dot(hi, spread) + dot(mid, spread) + dot(lo, spread)
-    coef_ref[...] = columns[:LEV]
-    rate_ref[...] = columns[LEV:]
+    columns = dot(
+        jnp.concatenate(split3(tail), axis=0).T,
+        jnp.concatenate([spread, spread, spread], axis=0),
+    )
+    coef_ref[...] = columns[begin : begin + LEV]
+    rate_ref[...] = columns[begin + LEV : begin + 2 * LEV]
     element, relative = neighbour_lanes(recv_ref, device)
     cuts = []
     for o, beyond in ((2, 4), (0, 0)):

time: 44.8 us -> 44.8 us (level)
  no operation moved by 1% of the time
where the time goes in v7:
time: 44.8 us; the launch traced here: 44.7 us
  blocking collectives  30.1 us (67%)
  Pallas kernels  5.87 us (13%)
  starting transfers between devices  5.27 us (12%)
  waiting for transfers between devices  2.72 us (6%)
  between operations  0.69 us (2%)
    all_to_all x1, blocking collectives, per_device(): lax.all_to_all(message.reshape(SPANS, 16, 128), 'curve', split_axis=0, co...  30.1 us
    ppermute x4, starting transfers between devices, swap(): lax.ppermute(x, 'curve', [(i, partner(i) % SPANS) for i in range(SPANS)])  5.27 us
    ppermute x4, waiting for transfers between devices, swap(): lax.ppermute(x, 'curve', [(i, partner(i) % SPANS) for i in range(SPANS)])  2.72 us
    pallas_call x1, Pallas kernels, per_device(): pl.pallas_call(span_kernel, out_shape=(shape((STATE, SLOT), f32), shape((...  2.03 us
    pallas_call x1, Pallas kernels, per_device(): pl.pallas_call(pack_kernel, out_shape=(shape((SLOT * CHUNKS, 128), f32),...  1.51 us
    pallas_call x1, Pallas kernels, per_device(): pl.pallas_call(beyond_kernel, out_shape=shape((NF, COL, LEV), f32), out_s...  1.12 us
  transfers between devices with their start and end apart: 4, of which 1 were waited for; matrix products, arithmetic and copies ran while one was open for 0% of the time, Pallas kernels for 6%

profile of v7, /device:TPU:1, one launch (start us, length us, event | category | flops | bytes accessed | tf_op | source)
XLA Modules:
  0.0 44.7 jit_solution(11801998948207475632)
XLA Ops:
  0.6 1.5 %pack.1 = (f32[1024,128]{1,0:T(8,128)S(1)}, s32[8,128]{1,0:T(8,128)S(1)}, f32[432,128]{1,0:T(8,128)S(1)}) custom-call(f32[12,64,72]{2,1,0:T(8,128)} %bitcast.14, s32[1,64]{1,0:T(1,128)} %bitcast.16, f32[72,128]{1,0:T(8,128)} %diff_ref.1, f32[72,128]{1,0:T(8,128)} %courant_ref.1, s32[1,128]{1,0:T(1,128)} %bitcast.12, s32[4,4]{1,0:T(4,128)} %near_hbm.1), custom_call_target="tpu_custom_call" | custom-call | tf_op jit(solution)/shard_map/pack/pallas_call | solution.py:383
  2.1 30.1 %all_to_all.5 = f32[64,16,128]{2,1,0:T(8,128)S(1)} all-to-all(f32[64,16,128]{2,1,0:T(8,128)S(1)} %bitcast.11), channel_id=1, replica_groups=mesh['curve'=64,'field'=4] {'curve'}, dimensions={0} | all-to-all | bytes 1048576 | tf_op jit(solution)/shard_map/all_to_all | solution.py:403
  32.3 0.7 %element.1 = (f32[432,128]{1,0:T(8,128)S(1)}, bf16[256,256]{1,0:T(8,128)(2,1)S(1)}) custom-call(f32[1024,128]{1,0:T(8,128)S(1)} %bitcast.9, s32[8,128]{1,0:T(8,128)S(1)} %get-tuple-element.16.slot_ref, f32[432,128]{1,0:T(8,128)S(1)} %get-tuple-element.17.x_ref), custom_call_target="tpu_custom_call" | custom-call | tf_op jit(solution)/shard_map/element/pallas_call | solution.py:408
  33.0 1.5 %collective-permute-start.2 = (f32[432,128]{1,0:T(8,128)S(1)}, f32[432,128]{1,0:T(8,128)S(1)}, u32[]{:S(2)}, u32[]{:S(2)}) collective-permute-start(f32[432,128]{1,0:T(8,128)S(1)} %get-tuple-element.24.own_ref.x_ref), channel_id=1, source_target_pairs={{0,252},{4,8},{8,4},{12,16},{16,12},{20,24},{24,20},{28,32},{32,28... | collective-permute-start | bytes 663560 | tf_op jit(solution)/shard_map/ppermute | solution.py:369
  34.5 0.0 copy-start
  34.5 0.0 copy-start.1
  34.5 0.0 copy-start.2
  34.5 0.2 cut.1
  34.7 0.0 copy-start.3
  34.7 0.8 %collective-permute-start.3 = (f32[432,128]{1,0:T(8,128)S(1)}, f32[432,128]{1,0:T(8,128)S(1)}, u32[]{:S(2)}, u32[]{:S(2)}) collective-permute-start(f32[432,128]{1,0:T(8,128)S(1)} %get-tuple-element.24.own_ref.x_ref), channel_id=1, source_target_pairs={{0,4},{4,0},{8,12},{12,8},{16,20},{20,16},{24,28},{28,24},{32,36},... | collective-permute-start | bytes 663560 | tf_op jit(solution)/shard_map/ppermute | solution.py:369
  35.5 3.0 %collective-permute-start = (f32[216,128]{1,0:T(8,128)S(1)}, f32[216,128]{1,0:T(8,128)S(1)}, u32[]{:S(2)}, u32[]{:S(2)}) collective-permute-start(f32[216,128]{1,0:T(8,128)S(1)} %get-tuple-element.21), channel_id=1, source_target_pairs={{0,248},{4,252},{8,16},{12,20},{16,8},{20,12},{24,32},{28,36},{32,... | collective-permute-start | bytes 331784 | tf_op jit(solution)/shard_map/ppermute | solution.py:369
  38.5 0.0 collective-permute-start.1
  38.5 0.0 copy-done
  38.5 0.0 copy-done.1
  38.5 0.0 copy-done.2
  38.5 0.0 copy-done.3
  38.5 2.0 %span.1 = (f32[864,128]{1,0:T(8,128)}, bf16[384,256]{1,0:T(8,128)(2,1)S(1)}, bf16[256,256]{1,0:T(8,128)(2,1)S(1)}, f32[432,128]{1,0:T(8,128)S(1)}) custom-call(f32[1024,128]{1,0:T(8,128)S(1)} %bitcast.10, f32[72,128]{1,0:T(8,128)S(1)} %copy-done, f32[72,128]{1,0:T(8,128)S(1)} %copy-done.1, s32[1,128]{1,0:T(1,128)S(1)} %bitcast.13, f32[64,64]{1,0:T(8,128)S(1)} %copy-done.2, ...), custom_call_target="tpu_custom_call" | custom-call | tf_op jit(solution)/shard_map/span/pallas_call | solution.py:431
  40.5 0.0 collective-permute-done.2.across_ref
  40.5 0.0 collective-permute-done.3.chip_ref
  40.5 0.3 beside.1.part_ref
  40.8 2.7 %collective-permute-done.far_ref = f32[216,128]{1,0:T(8,128)S(1)} collective-permute-done((f32[216,128]{1,0:T(8,128)S(1)}, f32[216,128]{1,0:T(8,128)S(1)}, u32[]{:S(2)}, u32[]{:S(2)}) %collective-permute-start) | collective-permute-done | bytes 110624 | tf_op jit(solution)/shard_map/ppermute | solution.py:369
  43.5 0.0 collective-permute-done.1.near_ref
  43.6 1.1 %beyond.1 = f32[12,64,72]{2,1,0:T(8,128)} custom-call(f32[216,128]{1,0:T(8,128)S(1)} %collective-permute-done.far_ref, f32[216,128]{1,0:T(8,128)S(1)} %collective-permute-done.1.near_ref, f32[432,128]{1,0:T(8,128)S(1)} %beside.1.part_ref, bf16[256,256]{1,0:T(8,128)(2,1)S(1)} %get-tuple-element.27.cut_ref), custom_call_target="tpu_custom_call" | custom-call | tf_op jit(solution)/shard_map/beyond/pallas_call | solution.py:451
Async XLA Ops:
  33.0 7.6 %collective-permute-start.2 = (f32[432,128]{1,0:T(8,128)S(1)}, f32[432,128]{1,0:T(8,128)S(1)}, u32[]{:S(2)}, u32[]{:S(2)}) collective-permute-start(f32[432,128]{1,0:T(8,128)S(1)} %get-tuple-element.24.own_ref.x_ref), channel_id=1, source_target_pairs={{0,252},{4,8},{8,4},{12,16},{16,12},{20,24},{24,20},{28,32},{32,28... | collective-permute-start | bytes 663560 | tf_op jit(solution)/shard_map/ppermute | solution.py:369
  34.5 4.0 %copy-start = (f32[72,128]{1,0:T(8,128)S(1)}, f32[72,128]{1,0:T(8,128)}, u32[]{:S(2)}) copy-start(f32[72,128]{1,0:T(8,128)} %diff_ref.1) | copy-start | bytes 110596
  34.5 4.0 %copy-start.1 = (f32[72,128]{1,0:T(8,128)S(1)}, f32[72,128]{1,0:T(8,128)}, u32[]{:S(2)}) copy-start(f32[72,128]{1,0:T(8,128)} %courant_ref.1) | copy-start | bytes 110596
  34.5 4.0 %copy-start.2 = (f32[64,64]{1,0:T(8,128)S(1)}, f32[64,64]{1,0:T(8,128)}, u32[]{:S(2)}) copy-start(f32[64,64]{1,0:T(8,128)} %constant.2.clone.lap_ref) | copy-start | bytes 49156
  34.7 3.8 %copy-start.3 = (s32[128]{0:T(128)S(1)}, s32[128]{0:T(128)}, u32[]{:S(2)}) copy-start(s32[128]{0:T(128)} %param.11) | copy-start | bytes 1540
  34.7 5.8 %collective-permute-start.3 = (f32[432,128]{1,0:T(8,128)S(1)}, f32[432,128]{1,0:T(8,128)S(1)}, u32[]{:S(2)}, u32[]{:S(2)}) collective-permute-start(f32[432,128]{1,0:T(8,128)S(1)} %get-tuple-element.24.own_ref.x_ref), channel_id=1, source_target_pairs={{0,4},{4,0},{8,12},{12,8},{16,20},{20,16},{24,28},{28,24},{32,36},... | collective-permute-start | bytes 663560 | tf_op jit(solution)/shard_map/ppermute | solution.py:369
  35.5 8.1 %collective-permute-start = (f32[216,128]{1,0:T(8,128)S(1)}, f32[216,128]{1,0:T(8,128)S(1)}, u32[]{:S(2)}, u32[]{:S(2)}) collective-permute-start(f32[216,128]{1,0:T(8,128)S(1)} %get-tuple-element.21), channel_id=1, source_target_pairs={{0,248},{4,252},{8,16},{12,20},{16,8},{20,12},{24,32},{28,36},{32,... | collective-permute-start | bytes 331784 | tf_op jit(solution)/shard_map/ppermute | solution.py:369
  38.5 5.1 %collective-permute-start.1 = (f32[216,128]{1,0:T(8,128)S(1)}, f32[216,128]{1,0:T(8,128)S(1)}, u32[]{:S(2)}, u32[]{:S(2)}) collective-permute-start(f32[216,128]{1,0:T(8,128)S(1)} %get-tuple-element.23), channel_id=1, source_target_pairs={{0,8},{4,12},{8,0},{12,4},{16,24},{20,28},{24,16},{28,20},{32,40},... | collective-permute-start | bytes 331784 | tf_op jit(solution)/shard_map/ppermute | solution.py:369

commit v8 on v6

--- a/solution.py
+++ b/solution.py
@@ -214,8 +214,9 @@
 
 def cut_kernel(x_ref, matrix_ref, near_ref, far_ref):
     half = PAIR * LEV // 2
-    hi, lo = split2(jnp.concatenate([x_ref[:half, :], x_ref[half:, :]], axis=1))
-    cut = dot(hi, matrix_ref[...]) + dot(lo, matrix_ref[...])
+    parts = split2(jnp.concatenate([x_ref[:half, :], x_ref[half:, :]], axis=1))
+    matrix = matrix_ref[...]
+    cut = dot(jnp.concatenate(parts, axis=1), jnp.concatenate([matrix, matrix], axis=0))
     near_ref[...] = cut[:, :128]
     far_ref[...] = cut[:, 128:]
 

time: 44.8 us -> 44.8 us (level)
  no operation moved by 1% of the time
where the time goes in v8:
time: 44.8 us; the launch traced here: 44.7 us
  blocking collectives  30.1 us (67%)
  Pallas kernels  5.91 us (13%)
  starting transfers between devices  5.27 us (12%)
  waiting for transfers between devices  2.72 us (6%)
  between operations  0.69 us (2%)
    all_to_all x1, blocking collectives, per_device(): lax.all_to_all(message.reshape(SPANS, 16, 128), 'curve', split_axis=0, co...  30.1 us
    ppermute x4, starting transfers between devices, swap(): lax.ppermute(x, 'curve', [(i, partner(i) % SPANS) for i in range(SPANS)])  5.27 us
    ppermute x4, waiting for transfers between devices, swap(): lax.ppermute(x, 'curve', [(i, partner(i) % SPANS) for i in range(SPANS)])  2.72 us
    pallas_call x1, Pallas kernels, per_device(): pl.pallas_call(span_kernel, out_shape=(shape((STATE, SLOT), f32), shape((...  2.03 us
    pallas_call x1, Pallas kernels, per_device(): pl.pallas_call(pack_kernel, out_shape=(shape((SLOT * CHUNKS, 128), f32),...  1.51 us
    pallas_call x1, Pallas kernels, per_device(): pl.pallas_call(beyond_kernel, out_shape=shape((NF, COL, LEV), f32), out_s...  1.12 us
  transfers between devices with their start and end apart: 4, of which 1 were waited for; matrix products, arithmetic and copies ran while one was open for 0% of the time, Pallas kernels for 6%

profile of v8, /device:TPU:1, one launch (start us, length us, event | category | flops | bytes accessed | tf_op | source)
XLA Modules:
  0.0 44.7 jit_solution(840333243286705387)
XLA Ops:
  0.6 1.5 %pack.1 = (f32[1024,128]{1,0:T(8,128)S(1)}, s32[8,128]{1,0:T(8,128)S(1)}, f32[432,128]{1,0:T(8,128)S(1)}) custom-call(f32[12,64,72]{2,1,0:T(8,128)} %bitcast.14, s32[1,64]{1,0:T(1,128)} %bitcast.16, f32[72,128]{1,0:T(8,128)} %diff_ref.1, f32[72,128]{1,0:T(8,128)} %courant_ref.1, s32[1,128]{1,0:T(1,128)} %bitcast.12, s32[4,4]{1,0:T(4,128)} %near_hbm.1), custom_call_target="tpu_custom_call" | custom-call | tf_op jit(solution)/shard_map/pack/pallas_call | solution.py:380
  2.1 30.1 %all_to_all.5 = f32[64,16,128]{2,1,0:T(8,128)S(1)} all-to-all(f32[64,16,128]{2,1,0:T(8,128)S(1)} %bitcast.11), channel_id=1, replica_groups=mesh['curve'=64,'field'=4] {'curve'}, dimensions={0} | all-to-all | bytes 1048576 | tf_op jit(solution)/shard_map/all_to_all | solution.py:400
  32.3 0.7 %element.1 = (f32[432,128]{1,0:T(8,128)S(1)}, bf16[256,256]{1,0:T(8,128)(2,1)S(1)}) custom-call(f32[1024,128]{1,0:T(8,128)S(1)} %bitcast.9, s32[8,128]{1,0:T(8,128)S(1)} %get-tuple-element.16.slot_ref, f32[432,128]{1,0:T(8,128)S(1)} %get-tuple-element.17.x_ref), custom_call_target="tpu_custom_call" | custom-call | tf_op jit(solution)/shard_map/element/pallas_call | solution.py:405
  33.0 1.5 %collective-permute-start.2 = (f32[432,128]{1,0:T(8,128)S(1)}, f32[432,128]{1,0:T(8,128)S(1)}, u32[]{:S(2)}, u32[]{:S(2)}) collective-permute-start(f32[432,128]{1,0:T(8,128)S(1)} %get-tuple-element.24.own_ref.x_ref), channel_id=1, source_target_pairs={{0,252},{4,8},{8,4},{12,16},{16,12},{20,24},{24,20},{28,32},{32,28... | collective-permute-start | bytes 663560 | tf_op jit(solution)/shard_map/ppermute | solution.py:366
  34.5 0.0 copy-start
  34.5 0.0 copy-start.1
  34.5 0.0 copy-start.2
  34.5 0.2 cut.1
  34.7 0.0 copy-start.3
  34.7 0.8 %collective-permute-start.3 = (f32[432,128]{1,0:T(8,128)S(1)}, f32[432,128]{1,0:T(8,128)S(1)}, u32[]{:S(2)}, u32[]{:S(2)}) collective-permute-start(f32[432,128]{1,0:T(8,128)S(1)} %get-tuple-element.24.own_ref.x_ref), channel_id=1, source_target_pairs={{0,4},{4,0},{8,12},{12,8},{16,20},{20,16},{24,28},{28,24},{32,36},... | collective-permute-start | bytes 663560 | tf_op jit(solution)/shard_map/ppermute | solution.py:366
  35.5 3.0 %collective-permute-start = (f32[216,128]{1,0:T(8,128)S(1)}, f32[216,128]{1,0:T(8,128)S(1)}, u32[]{:S(2)}, u32[]{:S(2)}) collective-permute-start(f32[216,128]{1,0:T(8,128)S(1)} %get-tuple-element.21), channel_id=1, source_target_pairs={{0,248},{4,252},{8,16},{12,20},{16,8},{20,12},{24,32},{28,36},{32,... | collective-permute-start | bytes 331784 | tf_op jit(solution)/shard_map/ppermute | solution.py:366
  38.5 0.0 collective-permute-start.1
  38.5 0.0 copy-done
  38.5 0.0 copy-done.1
  38.5 0.0 copy-done.2
  38.5 0.0 copy-done.3
  38.5 2.0 %span.1 = (f32[864,128]{1,0:T(8,128)}, bf16[384,256]{1,0:T(8,128)(2,1)S(1)}, bf16[256,256]{1,0:T(8,128)(2,1)S(1)}, f32[432,128]{1,0:T(8,128)S(1)}) custom-call(f32[1024,128]{1,0:T(8,128)S(1)} %bitcast.10, f32[72,128]{1,0:T(8,128)S(1)} %copy-done, f32[72,128]{1,0:T(8,128)S(1)} %copy-done.1, s32[1,128]{1,0:T(1,128)S(1)} %bitcast.13, f32[64,64]{1,0:T(8,128)S(1)} %copy-done.2, ...), custom_call_target="tpu_custom_call" | custom-call | tf_op jit(solution)/shard_map/span/pallas_call | solution.py:428
  40.6 0.0 collective-permute-done.2.across_ref
  40.6 0.0 collective-permute-done.3.chip_ref
  40.6 0.3 beside.1.part_ref
  40.9 2.7 %collective-permute-done.far_ref = f32[216,128]{1,0:T(8,128)S(1)} collective-permute-done((f32[216,128]{1,0:T(8,128)S(1)}, f32[216,128]{1,0:T(8,128)S(1)}, u32[]{:S(2)}, u32[]{:S(2)}) %collective-permute-start) | collective-permute-done | bytes 110624 | tf_op jit(solution)/shard_map/ppermute | solution.py:366
  43.6 0.0 collective-permute-done.1.near_ref
  43.6 1.1 %beyond.1 = f32[12,64,72]{2,1,0:T(8,128)} custom-call(f32[216,128]{1,0:T(8,128)S(1)} %collective-permute-done.far_ref, f32[216,128]{1,0:T(8,128)S(1)} %collective-permute-done.1.near_ref, f32[432,128]{1,0:T(8,128)S(1)} %beside.1.part_ref, bf16[256,256]{1,0:T(8,128)(2,1)S(1)} %get-tuple-element.27.cut_ref), custom_call_target="tpu_custom_call" | custom-call | tf_op jit(solution)/shard_map/beyond/pallas_call | solution.py:448
Async XLA Ops:
  33.0 7.6 %collective-permute-start.2 = (f32[432,128]{1,0:T(8,128)S(1)}, f32[432,128]{1,0:T(8,128)S(1)}, u32[]{:S(2)}, u32[]{:S(2)}) collective-permute-start(f32[432,128]{1,0:T(8,128)S(1)} %get-tuple-element.24.own_ref.x_ref), channel_id=1, source_target_pairs={{0,252},{4,8},{8,4},{12,16},{16,12},{20,24},{24,20},{28,32},{32,28... | collective-permute-start | bytes 663560 | tf_op jit(solution)/shard_map/ppermute | solution.py:366
  34.5 4.0 %copy-start = (f32[72,128]{1,0:T(8,128)S(1)}, f32[72,128]{1,0:T(8,128)}, u32[]{:S(2)}) copy-start(f32[72,128]{1,0:T(8,128)} %diff_ref.1) | copy-start | bytes 110596
  34.5 4.0 %copy-start.1 = (f32[72,128]{1,0:T(8,128)S(1)}, f32[72,128]{1,0:T(8,128)}, u32[]{:S(2)}) copy-start(f32[72,128]{1,0:T(8,128)} %courant_ref.1) | copy-start | bytes 110596
  34.5 4.0 %copy-start.2 = (f32[64,64]{1,0:T(8,128)S(1)}, f32[64,64]{1,0:T(8,128)}, u32[]{:S(2)}) copy-start(f32[64,64]{1,0:T(8,128)} %constant.2.clone.lap_ref) | copy-start | bytes 49156
  34.7 3.8 %copy-start.3 = (s32[128]{0:T(128)S(1)}, s32[128]{0:T(128)}, u32[]{:S(2)}) copy-start(s32[128]{0:T(128)} %param.11) | copy-start | bytes 1540
  34.7 5.8 %collective-permute-start.3 = (f32[432,128]{1,0:T(8,128)S(1)}, f32[432,128]{1,0:T(8,128)S(1)}, u32[]{:S(2)}, u32[]{:S(2)}) collective-permute-start(f32[432,128]{1,0:T(8,128)S(1)} %get-tuple-element.24.own_ref.x_ref), channel_id=1, source_target_pairs={{0,4},{4,0},{8,12},{12,8},{16,20},{20,16},{24,28},{28,24},{32,36},... | collective-permute-start | bytes 663560 | tf_op jit(solution)/shard_map/ppermute | solution.py:366
  35.5 8.1 %collective-permute-start = (f32[216,128]{1,0:T(8,128)S(1)}, f32[216,128]{1,0:T(8,128)S(1)}, u32[]{:S(2)}, u32[]{:S(2)}) collective-permute-start(f32[216,128]{1,0:T(8,128)S(1)} %get-tuple-element.21), channel_id=1, source_target_pairs={{0,248},{4,252},{8,16},{12,20},{16,8},{20,12},{24,32},{28,36},{32,... | collective-permute-start | bytes 331784 | tf_op jit(solution)/shard_map/ppermute | solution.py:366
  38.5 5.1 %collective-permute-start.1 = (f32[216,128]{1,0:T(8,128)S(1)}, f32[216,128]{1,0:T(8,128)S(1)}, u32[]{:S(2)}, u32[]{:S(2)}) collective-permute-start(f32[216,128]{1,0:T(8,128)S(1)} %get-tuple-element.23), channel_id=1, source_target_pairs={{0,8},{4,12},{8,0},{12,4},{16,24},{20,28},{24,16},{28,20},{32,40},... | collective-permute-start | bytes 331784 | tf_op jit(solution)/shard_map/ppermute | solution.py:366
